TPU v7x, 128 devices: a whole 4x4x4 slice. The times are simulated.
128 devices in a mesh: ctx: 64 (over z_lo, x, y, core), ch: 2 (over z_hi).
Axes of the slice: x: 4, y: 4, z: 4 (z_hi: 2, z_lo: 2; z = z_hi * 2 + z_lo), core: 2. Of those that a mesh axis runs over, the one named last changes fastest.
Arguments:
- q_proj: bfloat16 [8192, 4096], P('ctx', 'ch'), may hold values from -6 to 6
- k_proj: bfloat16 [8192, 4096], P('ctx', 'ch'), may hold values from -6 to 6
- v_proj: bfloat16 [8192, 4096], P('ctx', 'ch'), may hold values from -6 to 6
- filt: float32 [256, 256], P(None, 'ch'), may hold values from -3 to 3
- skip: float32 [4096], P('ch'), may hold values from 0.5 to 1.5
- grad_out: bfloat16 [8192, 4096], P('ctx', 'ch'), may hold values from -6 to 6
Outputs:
- mixed_out: bfloat16 [8192, 4096], P('ctx', 'ch')
- q_grad: bfloat16 [8192, 4096], P('ctx', 'ch')
- k_grad: bfloat16 [8192, 4096], P('ctx', 'ch')
- v_grad: bfloat16 [8192, 4096], P('ctx', 'ch')
- filt_grad: float32 [256, 256], P('ctx')
All inputs are finite; a program needn't handle non-finite values.
Results may differ from a plain program's by a relative error of at most 0.0054.
Values may be sent and summed in bfloat16 or wider, within the bound.
A program may use at most 192 MiB of HBM per device.

v0:
```python
import jax
import jax.numpy as jnp
from jax import lax
from jax.sharding import PartitionSpec as P


def passed_along(block, axis, distance):
    devices = range(lax.axis_size(axis))
    route = [(i - distance, i) for i in devices if i - distance in devices]
    return lax.ppermute(block, axis, route)


def shards(q_proj, k_proj, v_proj, filt, skip, grad_out):
    rows, width = q_proj.shape
    lags, groups = filt.shape
    group = width // groups
    qf = q_proj.astype(jnp.float32)
    kf = k_proj.astype(jnp.float32)
    vf = v_proj.astype(jnp.float32)
    gf = grad_out.astype(jnp.float32)
    stream = (kf * vf).astype(jnp.bfloat16)
    dconv = (gf * qf).astype(jnp.bfloat16)
    taps = filt.astype(jnp.bfloat16)
    padded_taps = jnp.pad(taps.T, ((0, 0), (rows, 4 * rows)))

    def layout(array):
        return array.reshape(rows, groups, group).transpose(1, 2, 0)

    def restore(array):
        return array.transpose(2, 0, 1).reshape(rows, width)

    earlier = [layout(stream)]
    current = stream
    for step in range(2):
        current = passed_along(current, "ctx", 1)
        earlier.append(layout(current))
    dconv_lay = layout(dconv)
    conv = jnp.zeros((groups, group, rows), jnp.float32)
    adjoint_terms = []
    for block in range(3):
        segment = lax.slice_in_dim(
            padded_taps, block * rows + 1, block * rows + 1 + 2 * rows, axis=1
        )
        spread = jnp.broadcast_to(segment[:, None, :], (groups, rows, 2 * rows)).reshape(
            groups, 2 * rows * rows
        )
        table_skewed = spread[:, : rows * (2 * rows - 1)].reshape(groups, rows, 2 * rows - 1)
        tab = table_skewed[:, :, rows - 1 :]
        conv = conv + jnp.einsum(
            "grs,gkr->gks", tab, earlier[block], preferred_element_type=jnp.float32
        )
        adjoint_terms.append(
            jnp.einsum("grs,gks->gkr", tab, dconv_lay, preferred_element_type=jnp.float32)
        )
    reversed_blocks = jnp.concatenate([earlier[block][:, :, ::-1] for block in range(3)], axis=2)
    outer = jnp.einsum(
        "gks,gkc->gsc", dconv_lay, reversed_blocks, preferred_element_type=jnp.float32
    )
    widened = jnp.pad(outer, ((0, 0), (0, 0), (0, rows)))
    skewed = widened.reshape(groups, 4 * rows * rows)[:, : rows * (4 * rows - 1)].reshape(
        groups, rows, 4 * rows - 1
    )
    diagonals = jnp.sum(skewed, axis=1)
    carried = adjoint_terms[2]
    for step in range(2):
        carried = passed_along(carried, "ctx", -1)
        if step == 0:
            carried = carried + adjoint_terms[1]
    dstream = adjoint_terms[0] + carried
    conv = restore(conv) + skip[None, :] * stream.astype(jnp.float32)
    mixed_out = (qf * conv).astype(jnp.bfloat16)
    q_grad = (gf * conv).astype(jnp.bfloat16)
    dstream = restore(dstream) + skip[None, :] * dconv.astype(jnp.float32)
    k_grad = (dstream * vf).astype(jnp.bfloat16)
    v_grad = (dstream * kf).astype(jnp.bfloat16)
    filter_terms = diagonals[:, rows - 1 : rows - 1 + lags].T
    summed = lax.psum_scatter(filter_terms, "ctx", scatter_dimension=0, tiled=True)
    summed = summed / jnp.sqrt(jnp.float32(group * rows * lax.axis_size("ctx")))
    filt_grad = lax.all_gather(summed, "ch", axis=1, tiled=True)
    return (mixed_out, q_grad, k_grad, v_grad, filt_grad)


def solution(mesh):
    in_specs = (
        P("ctx", "ch"),
        P("ctx", "ch"),
        P("ctx", "ch"),
        P(None, "ch"),
        P("ch"),
        P("ctx", "ch"),
    )
    out_specs = (P("ctx", "ch"), P("ctx", "ch"), P("ctx", "ch"), P("ctx", "ch"), P("ctx", None))
    return jax.shard_map(shards, mesh=mesh, in_specs=in_specs, out_specs=out_specs, check_vma=False)
```

profile of v0, /device:TPU:1, one launch (start us, length us, event | category | flops | bytes accessed | tf_op | source)
XLA Modules:
  0.0 843.1 jit_solution(17161200388697066066)
XLA Ops:
  10.2 4.6 collective-permute-start
  19.7 12.3 %copy.43 = bf16[16,8,128,256]{3,1,2,0:T(8,128)(2,1)} copy(bf16[16,8,128,256]{3,2,1,0:T(8,128)(2,1)} %bitcast.52) | data formatting | bytes 16777216
  32.0 7.1 slice.44
  39.2 29.6 %reshape.58 = bf16[128,128,255]{2,1,0:T(8,128)(2,1)} reshape(bf16[128,32640]{1,0:T(8,128)(2,1)} %slice.44) | data formatting | bytes 16711680 | tf_op jit(solution)/shard_map/reshape | solution.py:47
  70.8 4.9 fusion.10
  80.6 12.3 %copy.44 = bf16[16,8,128,256]{3,1,2,0:T(8,128)(2,1)} copy(bf16[16,8,128,256]{3,2,1,0:T(8,128)(2,1)} %bitcast.53) | data formatting | bytes 16777216
  93.0 7.1 slice.46
  100.1 29.7 %reshape.61 = bf16[128,128,255]{2,1,0:T(8,128)(2,1)} reshape(bf16[128,32640]{1,0:T(8,128)(2,1)} %slice.46) | data formatting | bytes 16711680 | tf_op jit(solution)/shard_map/reshape | solution.py:47
  133.7 12.3 %copy.45 = bf16[16,8,128,256]{3,1,2,0:T(8,128)(2,1)} copy(bf16[16,8,128,256]{3,2,1,0:T(8,128)(2,1)} %bitcast.54) | data formatting | bytes 16777216
  146.1 7.1 slice.48
  153.2 29.9 %reshape.64 = bf16[128,128,255]{2,1,0:T(8,128)(2,1)} reshape(bf16[128,32640]{1,0:T(8,128)(2,1)} %slice.48) | data formatting | bytes 16711680 | tf_op jit(solution)/shard_map/reshape | solution.py:47
  184.2 5.1 fusion.18
  190.0 5.1 fusion.24
  204.8 11.5 %collective-permute-done.2 = f32[128,16,128]{2,1,0:T(8,128)} collective-permute-done((f32[128,16,128]{2,1,0:T(8,128)}, f32[128,16,128]{2,1,0:T(8,128)}, u32[]{:S(2)}, u32[]{:S(2)}) %collective-permute-start.2) | collective-permute-done | bytes 1048608 | tf_op jit(solution)/shard_map/ppermute | solution.py:10
  216.2 7.0 fusion.21
  225.2 10.3 %fusion.12 = f32[128,128,384]{2,1,0:T(8,128)} fusion(bf16[128,16,128]{2,1,0:T(8,128)(2,1)S(1)} %bitcast.60, bf16[128,16,128]{2,1,0:T(8,128)(2,1)S(1)} %rev.11, bf16[128,16,128]{2,1,0:T(8,128)(2,1)S(1)} %rev.10, bf16[128,16,128]{2,1,0:T(8,128)(2,1)S(1)} %rev.9), kind=kOutput, calls=%fused_computation.12 | convolution fusion | flops 206045184 | bytes 27262976 | tf_op jit(solution)/shard_map/gks,gkc->gsc/dot_general | solution.py:56
  235.4 11.5 %pad.9 = f32[128,128,512]{2,1,0:T(8,128)S(1)} pad(f32[128,128,384]{2,1,0:T(8,128)} %fusion.12, f32[]{:T(128)} %constant.7.clone.1), padding=0_0x0_0x0_128 | pad | bytes 58720260 | tf_op jit(solution)/shard_map/jit(_pad)/pad | solution.py:59
  246.9 21.5 %copy.46 = f32[16,8,128,512]{3,1,2,0:T(8,128)} copy(f32[16,8,128,512]{3,2,1,0:T(8,128)S(1)} %bitcast.48) | data formatting | bytes 67108864
  268.5 22.6 %slice.50 = f32[128,65408]{1,0:T(8,128)} slice(f32[128,65536]{1,0:T(8,128)} %bitcast.49), slice={[0:128], [0:65408]} | slice | bytes 66977792 | tf_op jit(solution)/shard_map/slice | solution.py:60
  291.0 35.4 %reshape.69 = f32[128,128,511]{2,1,0:T(8,128)} reshape(f32[128,65408]{1,0:T(8,128)} %slice.50) | data formatting | bytes 66977792 | tf_op jit(solution)/shard_map/reshape | solution.py:60
  326.5 13.0 %reduce_sum.9 = f32[128,511]{1,0:T(8,128)S(1)} reduce(f32[128,128,511]{2,1,0:T(8,128)} %reshape.69, f32[]{:T(128)} %constant.7.clone.1), dimensions={1}, to_apply=%region_0.1 | reduce | flops 8306816 | bytes 33750532 | tf_op jit(solution)/shard_map/reduce_sum | solution.py:63
  340.4 5.7 fusion.8
  349.2 477.1 %all-reduce.5.cloned.1.call-done = f32[256,128]{1,0:T(8,128)} async-done(((f32[256,128]{1,0:T(8,128)}), f32[256,128]{1,0:T(8,128)}) %all-reduce.5.cloned.1.call-update) | async-done | bytes 131088
  827.0 4.7 all_gather.3
  (66 shorter events, 40.4 us)
Async XLA Ops:
  7.2 819.1 %all-reduce.5.cloned.1.call-start = ((), (), s32[]{:S(2)}) async-start(), calls=%async_computation | async-start | bytes 262144
  8.5 23.5 %copy-start = (bf16[128,2048]{0,1:T(8,128)(2,1)}, bf16[128,2048]{0,1:T(8,128)(2,1)S(1)}, u32[]{:S(2)}) copy-start(bf16[128,2048]{0,1:T(8,128)(2,1)S(1)} %copy.33) | copy-start | bytes 1572868
  10.0 22.0 %copy-start.2 = (bf16[128,2048]{0,1:T(8,128)(2,1)}, bf16[128,2048]{0,1:T(8,128)(2,1)S(1)}, u32[]{:S(2)}) copy-start(bf16[128,2048]{0,1:T(8,128)(2,1)S(1)} %copy.32) | copy-start | bytes 1572868
  10.2 58.5 %collective-permute-start = (bf16[128,2048]{0,1:T(8,128)(2,1)S(1)}, bf16[128,2048]{0,1:T(8,128)(2,1)S(1)}, u32[]{:S(2)}, u32[]{:S(2)}) collective-permute-start(bf16[128,2048]{0,1:T(8,128)(2,1)S(1)} %fusion.29), channel_id=1, source_target_pairs={{0,2},{2,4},{4,6},{6,8},{8,10},{10,12},{12,14},{14,16},{16,18},{18... | collective-permute-start | bytes 1572872 | tf_op jit(solution)/shard_map/ppermute | solution.py:10
  39.2 36.6 %copy-start.8 = (bf16[128,2048]{1,0:T(8,128)(2,1)S(1)}, bf16[128,2048]{1,0:T(8,128)(2,1)}, u32[]{:S(2)}) copy-start(bf16[128,2048]{1,0:T(8,128)(2,1)} %param.11) | copy-start | bytes 1572868
  68.7 120.5 %collective-permute-start.1 = (bf16[128,2048]{0,1:T(8,128)(2,1)S(1)}, bf16[128,2048]{0,1:T(8,128)(2,1)S(1)}, u32[]{:S(2)}, u32[]{:S(2)}) collective-permute-start(bf16[128,2048]{0,1:T(8,128)(2,1)S(1)} %collective-permute-done), channel_id=1, source_target_pairs={{0,2},{2,4},{4,6},{6,8},{8,10},{10,12},{12,14},{14,16},{16,18},{18... | collective-permute-start | bytes 1572872 | tf_op jit(solution)/shard_map/ppermute | solution.py:10
  153.2 29.9 %copy-start.9 = (bf16[128,2048]{1,0:T(8,128)(2,1)S(1)}, bf16[128,2048]{1,0:T(8,128)(2,1)}, u32[]{:S(2)}) copy-start(bf16[128,2048]{1,0:T(8,128)(2,1)} %param.6) | copy-start | bytes 1572868
  183.1 12.0 %copy-start.10 = (f32[2048]{0:T(1024)S(1)}, f32[2048]{0:T(1024)}, u32[]{:S(2)}) copy-start(f32[2048]{0:T(1024)} %param.10) | copy-start | bytes 24580
  184.1 11.0 %copy-start.6 = (bf16[128,2048]{0,1:T(8,128)(2,1)S(1)}, bf16[128,2048]{0,1:T(8,128)(2,1)}, u32[]{:S(2)}) copy-start(bf16[128,2048]{0,1:T(8,128)(2,1)} %copy.37) | copy-start | bytes 1572868
  184.2 11.0 %copy-start.7 = (bf16[128,2048]{0,1:T(8,128)(2,1)S(1)}, bf16[128,2048]{0,1:T(8,128)(2,1)}, u32[]{:S(2)}) copy-start(bf16[128,2048]{0,1:T(8,128)(2,1)} %copy.31) | copy-start | bytes 1572868
  184.2 12.3 %slice-start = ((s8[8388608]{0:T(1024)(128)(4,1)}), s8[4194304]{0:T(1024)(128)(4,1)S(1)}, s32[]{:S(2)}) async-start(s8[8388608]{0:T(1024)(128)(4,1)} %bitcast.50), calls=%async_computation.1 | async-start | bytes 8388608
  189.2 0.8 copy-start.4
  190.0 6.4 slice-start.1
  190.0 12.6 %copy-start.11 = (u32[128]{0:T(128)S(1)}, u32[128]{0:T(128)}, u32[]{:S(2)}) copy-start(u32[128]{0:T(128)} %constant.15) | copy-start | bytes 1540
  195.2 9.2 %copy-start.5 = (bf16[128,2048]{0,1:T(8,128)(2,1)S(1)}, bf16[128,2048]{0,1:T(8,128)(2,1)}, u32[]{:S(2)}) copy-start(bf16[128,2048]{0,1:T(8,128)(2,1)} %copy-done.4) | copy-start | bytes 1572868
  199.8 16.4 %collective-permute-start.2 = (f32[128,16,128]{2,1,0:T(8,128)}, f32[128,16,128]{2,1,0:T(8,128)}, u32[]{:S(2)}, u32[]{:S(2)}) collective-permute-start(f32[128,16,128]{2,1,0:T(8,128)} %fusion), channel_id=1, source_target_pairs={{2,0},{4,2},{6,4},{8,6},{10,8},{12,10},{14,12},{16,14},{18,16},{20... | collective-permute-start | bytes 3145736 | tf_op jit(solution)/shard_map/ppermute | solution.py:10
  223.3 608.4 %collective-permute-start.3 = (f32[128,16,128]{2,1,0:T(8,128)}, f32[128,16,128]{2,1,0:T(8,128)}, u32[]{:S(2)}, u32[]{:S(2)}) collective-permute-start(f32[128,16,128]{2,1,0:T(8,128)} %fusion.21), channel_id=1, source_target_pairs={{2,0},{4,2},{6,4},{8,6},{10,8},{12,10},{14,12},{16,14},{18,16},{20... | collective-permute-start | bytes 3145736 | tf_op jit(solution)/shard_map/ppermute | solution.py:10
  339.5 493.5 %copy-start.1 = (bf16[128,2048]{0,1:T(8,128)(2,1)S(1)}, bf16[128,2048]{0,1:T(8,128)(2,1)}, u32[]{:S(2)}) copy-start(bf16[128,2048]{0,1:T(8,128)(2,1)} %copy-done) | copy-start | bytes 1572868
  339.5 493.5 %copy-start.3 = (bf16[128,2048]{0,1:T(8,128)(2,1)S(1)}, bf16[128,2048]{0,1:T(8,128)(2,1)}, u32[]{:S(2)}) copy-start(bf16[128,2048]{0,1:T(8,128)(2,1)} %copy-done.2) | copy-start | bytes 1572868
Sparse Core Ops, SparseCore 0:
  340.5 485.7 all-reduce.4
where the time goes:
time: 854 us; the launch traced here: 843 us
  waiting for transfers between devices  489 us (57%)
  local copies, waits for them, and re-layouts  264 us (31%)
  matrix products  41.5 us (5%)
  other arithmetic  17.8 us (2%)
  between operations  15.1 us (2%)
  starting transfers between devices  11 us (1%)
    unnamed x2, waiting for transfers between devices  477 us
    reshape x3, local copies, waits for them, and re-layouts, shards(): spread[:, :rows * (2 * rows - 1)].reshape(groups, rows, 2 * rows - 1)  89.2 us
    unnamed x42, local copies, waits for them, and re-layouts  70.5 us
    reshape x1, local copies, waits for them, and re-layouts, shards(): widened.reshape(groups, 4 * rows * rows)[:, :rows * (4 * rows - 1)]  35.4 us
    slice x1, local copies, waits for them, and re-layouts, shards(): widened.reshape(groups, 4 * rows * rows)[:, :rows * (4 * rows - 1)]  22.6 us
    slice x3, local copies, waits for them, and re-layouts, shards(): spread[:, :rows * (2 * rows - 1)].reshape(groups, rows, 2 * rows - 1)  21.4 us
  transfers between devices with their start and end apart: 5, of which 2 were waited for; matrix products, arithmetic and copies ran while one was open for 35% of the time, Pallas kernels for 0%

commit v1 on v0

v1 whole, which is shorter than its diff:
```python
import functools

import jax
import jax.numpy as jnp
from jax import lax
from jax.experimental import pallas as pl
from jax.experimental.pallas import tpu as pltpu
from jax.sharding import PartitionSpec as P

MESH = pl.DeviceIdType.MESH
F32 = jnp.float32
BF16 = jnp.bfloat16
ROWS = 128
LANES = 2048
TILES = LANES // 128
CHUNKS = 4
PER = TILES // CHUNKS
BLK = 16
NB = ROWS // BLK
TAPS = 256
SPAN = TAPS // BLK + 1
SLOTS = SPAN + 2 * (NB - 1)


def iota(shape, dim):
    return lax.broadcasted_iota(jnp.int32, shape, dim)


def lane_slice(tile, width=128):
    return pl.ds(pl.multiple_of(tile * 128, 128), width)


def kernel(
    n_ctx, scale,
    q_hbm, k_hbm, v_hbm, filt_ref, skip_ref, g_hbm,
    mo_hbm, qg_hbm, kg_hbm, vg_hbm, fg_ref,
    q_ref, k_ref, v_ref, g_ref,
    x_ref, dc_ref, s_ref, o_ref, mask_ref, sh_ref,
    d_ref, d1_ref, r1_ref, a1_ref, r2_ref,
    mo_ref, qg_ref, kg_ref, vg_ref,
    in_sem, out_sem, far_send, far_recv, near_send, near_recv,
    s1_send, s1_recv, s2_send, s2_recv, self_sem,
):
    d = lax.axis_index("ctx")
    h = lax.axis_index("ch")
    up = lax.rem(d + 2, n_ctx)
    down = lax.rem(d + n_ctx - 2, n_ctx)
    core = lax.rem(d, 2)
    mate = d + 1 - 2 * core
    zx = lax.div(d, 8)
    j = lax.rem(d, 8)
    y = lax.div(j, 2)
    n_zx = n_ctx // 8
    n_q = n_zx // 2
    base = zx * 8
    to_self = lax.rem(zx, 2) == core

    ins = []
    for c in range(CHUNKS):
        cols = pl.ds(c * PER * 128, PER * 128)
        row = []
        for n, (src, dst) in enumerate(((k_hbm, k_ref), (v_hbm, v_ref), (g_hbm, g_ref), (q_hbm, q_ref))):
            cp = pltpu.make_async_copy(src.at[:, cols], dst.at[:, cols], in_sem.at[n, c])
            cp.start()
            row.append(cp)
        ins.append(row)

    barrier = pltpu.get_barrier_semaphore()
    for other in (up, down):
        pl.semaphore_signal(barrier, inc=1, device_id=(other, h), device_id_type=MESH)
    for step in range(1, 8):
        other = base + lax.rem(j + step, 8)
        pl.semaphore_signal(barrier, inc=1, device_id=(other, h), device_id_type=MESH)
    for zz in range(n_zx):
        for hh in range(2):
            other = zz * 8 + y * 2 + lax.rem(zx, 2)

            @pl.when(jnp.logical_or(other != d, h != hh))
            def _():
                pl.semaphore_signal(barrier, inc=1, device_id=(other, hh), device_id_type=MESH)

    flip = (iota((ROWS, ROWS), 0) + iota((ROWS, ROWS), 1) == ROWS - 1).astype(F32).astype(BF16)
    fr, fc = iota((ROWS, 2 * ROWS), 0), iota((ROWS, 2 * ROWS), 1) % ROWS
    flip2 = (jnp.logical_and(fr // BLK == fc // BLK, fr % BLK + fc % BLK == BLK - 1)).astype(F32).astype(BF16)
    for g in range(8):
        mask_ref[g] = (iota((BLK, 128), 1) // BLK == g).astype(F32).astype(BF16)

    def far(n, c):
        ref, target, slot = ((x_ref, up, 2), (dc_ref, down, 2))[n]
        cs = pl.ds(c * PER, PER)
        return pltpu.make_async_remote_copy(
            src_ref=ref.at[0, cs], dst_ref=ref.at[slot, cs],
            send_sem=far_send.at[n, c], recv_sem=far_recv.at[n, c],
            device_id=(target, h), device_id_type=MESH,
        )

    def near(n, c, src_slot):
        ref = (x_ref, dc_ref)[n]
        cs = pl.ds(c * PER, PER)
        return pltpu.make_async_remote_copy(
            src_ref=ref.at[src_slot, cs], dst_ref=ref.at[1, cs],
            send_sem=near_send.at[n, c], recv_sem=near_recv.at[n, c],
            device_id=(mate, h), device_id_type=MESH,
        )

    for c in range(CHUNKS):
        for cp in ins[c]:
            cp.wait()

        def gate(n, carry):
            ls = lane_slice(n)
            st = (k_ref[:, ls].astype(F32) * v_ref[:, ls].astype(F32)).astype(BF16)
            dc_ref[0, n] = (g_ref[:, ls].astype(F32) * q_ref[:, ls].astype(F32)).astype(BF16)
            x_ref[0, n] = jnp.dot(flip, st, preferred_element_type=F32).astype(BF16)
            return carry

        lax.fori_loop(c * PER, (c + 1) * PER, gate, 0)
        if c == 0:
            pl.semaphore_wait(barrier, 9 + 2 * n_zx - to_self.astype(jnp.int32))
        far(0, c).start()
        far(1, c).start()

        @pl.when(core == 0)
        def _():
            near(0, c, 0).start()

        @pl.when(core == 1)
        def _():
            near(1, c, 0).start()

    s_ref[...] = jnp.zeros_like(s_ref)
    sh_ref[...] = jnp.zeros_like(sh_ref)
    taps = filt_ref[...].astype(BF16)
    ln = iota((288, 128), 1) % BLK

    def table(n, carry):
        e = (iota((128, 128), 0) == 8 * n + iota((128, 128), 1) // BLK).astype(F32).astype(BF16)
        f = jnp.dot(taps, e, preferred_element_type=F32)
        z = jnp.concatenate([jnp.zeros((16, 128), F32), f, jnp.zeros((16, 128), F32)], axis=0)
        amt = 15 - ln
        for b in (8, 4, 2, 1):
            sh_ref[8:296] = z
            z = jnp.where((amt & b) != 0, sh_ref[8 - b : 296 - b], z)
        zb = z.astype(BF16)
        for u in range(SPAN):
            s_ref[n, :, (NB - 1 + u) * 128 : (NB + u) * 128] = zb[16 + 16 * u : 32 + 16 * u]
        return carry

    lax.fori_loop(0, TILES, table, 0)

    def spread(block):
        n_u = block.shape[0] // BLK
        wide = block.reshape(n_u, 1, BLK, 128) * mask_ref[...][None]
        return wide.reshape(n_u * 128, 128)

    def operator(n, u0, n_u):
        return jnp.concatenate(
            [s_ref[n, :, (NB - 1 - i + u0) * 128 : (NB - 1 - i + u0 + n_u) * 128] for i in range(NB)], axis=0
        )

    def own(n, carry):
        rhs = jnp.concatenate([spread(x_ref[0, n]), spread(dc_ref[0, n])], axis=1)
        o_ref[n] = jnp.dot(operator(n, 0, NB), rhs, preferred_element_type=F32)
        return carry

    lax.fori_loop(0, TILES, own, 0)
    d_ref[...] = jnp.zeros_like(d_ref)

    ln2 = 15 - iota((264, 128), 1) % BLK

    def filter_terms(n, carry):
        dc = jnp.concatenate([dc_ref[0, n], dc_ref[1, n], dc_ref[2, n]], axis=0)
        lhs = jnp.concatenate([dc[BLK * i : BLK * i + SPAN * BLK] for i in range(NB)], axis=1)
        st = spread(x_ref[0, n])
        rhs = jnp.concatenate([st[(NB - 1 - i) * 128 : (NB - i) * 128] for i in range(NB)], axis=1)
        z = lax.dot_general(lhs, rhs, (((1,), (1,)), ((), ())), preferred_element_type=F32)
        sh_ref[0:272] = z
        z = jnp.where((ln2 & 8) != 0, sh_ref[8:272], z[:264])
        for b in (4, 2, 1):
            sh_ref[0:264] = z
            z = jnp.where((ln2 & b) != 0, sh_ref[b : 264 + b], z)
        z = z[:TAPS]
        hi = z.astype(BF16)
        lo = (z - hi.astype(F32)).astype(BF16)
        gr = iota((256, 128), 0) % 128
        g = (iota((256, 128), 1) == 8 * n + gr // BLK).astype(F32).astype(BF16)
        d_ref[...] += jnp.dot(jnp.concatenate([hi, lo], axis=1), g, preferred_element_type=F32)
        return carry

    def rest(n, carry):
        rx = jnp.concatenate([spread(x_ref[1, n]), spread(x_ref[2, n])], axis=0)
        rd = jnp.concatenate([spread(dc_ref[1, n]), spread(dc_ref[2, n])], axis=0)
        out = o_ref[n] + jnp.dot(
            operator(n, NB, 2 * NB), jnp.concatenate([rx, rd], axis=1), preferred_element_type=F32
        )
        ls = lane_slice(n)
        conv = jnp.concatenate([out[BLK * (NB - 1 - i) : BLK * (NB - i), :128] for i in range(NB)], axis=0)
        ds = out[:, 128:]
        hi = ds.astype(BF16)
        lo = (ds - hi.astype(F32)).astype(BF16)
        ds = jnp.dot(flip2, jnp.concatenate([hi, lo], axis=0), preferred_element_type=F32)
        kf, vf = k_ref[:, ls].astype(F32), v_ref[:, ls].astype(F32)
        qf, gf = q_ref[:, ls].astype(F32), g_ref[:, ls].astype(F32)
        skip = skip_ref[:, ls]
        conv = conv + skip * (kf * vf).astype(BF16).astype(F32)
        ds = ds + skip * dc_ref[0, n].astype(F32)
        mo_ref[:, ls] = (qf * conv).astype(BF16)
        qg_ref[:, ls] = (gf * conv).astype(BF16)
        kg_ref[:, ls] = (ds * vf).astype(BF16)
        vg_ref[:, ls] = (ds * kf).astype(BF16)
        return carry

    outs = []

    def finish(c):
        lax.fori_loop(c * PER, (c + 1) * PER, rest, 0)
        cols = pl.ds(c * PER * 128, PER * 128)
        for n, (src, dst) in enumerate(((mo_ref, mo_hbm), (qg_ref, qg_hbm), (kg_ref, kg_hbm), (vg_ref, vg_hbm))):
            cp = pltpu.make_async_copy(src.at[:, cols], dst.at[:, cols], out_sem.at[n, c])
            cp.start()
            outs.append(cp)

    def stage1(step):
        other = lax.rem(j + step, 8)
        return pltpu.make_async_remote_copy(
            src_ref=d1_ref.at[other], dst_ref=r1_ref.at[j],
            send_sem=s1_send.at[step], recv_sem=s1_recv.at[j],
            device_id=(base + other, h), device_id_type=MESH,
        )

    def stage1_arrival(step):
        other = lax.rem(j + step, 8)
        return pltpu.make_async_remote_copy(
            src_ref=d1_ref.at[other], dst_ref=r1_ref.at[other],
            send_sem=s1_send.at[step], recv_sem=s1_recv.at[other],
            device_id=(base + other, h), device_id_type=MESH,
        )

    for c in range(CHUNKS + 1):
        if c < CHUNKS:
            cs = pl.ds(c * PER, PER)
            far(0, c).wait_recv()
            far(1, c).wait_recv()

            @pl.when(d < 2)
            def _():
                x_ref[2, cs] = jnp.zeros((PER, 128, 128), BF16)

            @pl.when(d >= n_ctx - 2)
            def _():
                dc_ref[2, cs] = jnp.zeros((PER, 128, 128), BF16)

            @pl.when(core == 1)
            def _():
                near(0, c, 2).start()

            @pl.when(core == 0)
            def _():
                near(1, c, 2).start()

        if c > 0:
            near(0, c - 1, 0).wait_recv()
            near(1, c - 1, 0).wait_recv()
            lax.fori_loop((c - 1) * PER, c * PER, filter_terms, 0)
            if c == CHUNKS:
                for yy in range(4):
                    for cc in range(2):
                        for qq in range(n_q):
                            m = (2 * qq + cc) * 4 + yy
                            d1_ref[yy * 2 + cc, qq] = d_ref[8 * m : 8 * m + 8]
                for step in range(1, 8):
                    stage1(step).start()
            finish(c - 1)

    total = d1_ref[j]
    for step in range(1, 8):
        stage1_arrival(step).wait_recv()
        total = total + r1_ref[lax.rem(j + step, 8)]
    a1_ref[...] = total * scale

    def stage2(qq, cc, hh):
        n = (qq * 2 + cc) * 2 + hh
        target = (2 * qq + core) * 8 + y * 2 + cc
        return n, target, pltpu.make_async_remote_copy(
            src_ref=a1_ref.at[qq], dst_ref=r2_ref.at[zx * 2 + h],
            send_sem=s2_send.at[n], recv_sem=s2_recv.at[zx * 2 + h],
            device_id=(target, hh), device_id_type=MESH,
        )

    for qq in range(n_q):
        for cc in range(2):
            for hh in range(2):
                n, target, cp = stage2(qq, cc, hh)
                mine = jnp.logical_and(target == d, h == hh)

                @pl.when(jnp.logical_not(mine))
                def _():
                    cp.start()

                @pl.when(mine)
                def _():
                    r2_ref[zx * 2 + h] = a1_ref[qq]

    for zz in range(n_zx):
        for hh in range(2):
            other = zz * 8 + y * 2 + lax.rem(zx, 2)

            @pl.when(jnp.logical_or(other != d, h != hh))
            def _():
                pltpu.make_async_remote_copy(
                    src_ref=a1_ref.at[0], dst_ref=r2_ref.at[zz * 2 + hh],
                    send_sem=s2_send.at[0], recv_sem=s2_recv.at[zz * 2 + hh],
                    device_id=(other, hh), device_id_type=MESH,
                ).wait_recv()

    for hh in range(2):
        total = r2_ref[hh]
        for zz in range(1, n_zx):
            total = total + r2_ref[zz * 2 + hh]
        fg_ref[:, hh * 128 : (hh + 1) * 128] = jnp.where(core == 0, total[:4], total[4:])

    for cp in outs:
        cp.wait()
    for c in range(CHUNKS):
        for n in range(2):
            far(n, c).wait_send()
            near(n, c, 0).wait_send()
    for step in range(1, 8):
        stage1(step).wait_send()
    for qq in range(n_q):
        for cc in range(2):
            for hh in range(2):
                n, target, cp = stage2(qq, cc, hh)

                @pl.when(jnp.logical_or(target != d, h != hh))
                def _():
                    cp.wait_send()


def shards(q_proj, k_proj, v_proj, filt, skip, grad_out):
    n_ctx = lax.axis_size("ctx")
    scale = 1.0 / (16.0 * ROWS * n_ctx) ** 0.5
    any_spec = pl.BlockSpec(memory_space=pl.ANY)
    vmem = pl.BlockSpec(memory_space=pltpu.VMEM)
    big = jax.ShapeDtypeStruct((ROWS, LANES), BF16)
    n_q = n_ctx // 16
    outs = pl.pallas_call(
        functools.partial(kernel, n_ctx, scale),
        out_shape=(big, big, big, big, jax.ShapeDtypeStruct((4, 256), F32)),
        in_specs=[any_spec, any_spec, any_spec, vmem, vmem, any_spec],
        out_specs=(any_spec, any_spec, any_spec, any_spec, vmem),
        scratch_shapes=[pltpu.VMEM((ROWS, LANES), BF16)] * 4
        + [
            pltpu.VMEM((3, TILES, ROWS, 128), BF16),
            pltpu.VMEM((3, TILES, ROWS, 128), BF16),
            pltpu.VMEM((TILES, BLK, SLOTS * 128), BF16),
            pltpu.VMEM((TILES, ROWS, 256), F32),
            pltpu.VMEM((8, BLK, 128), BF16),
            pltpu.VMEM((304, 128), F32),
            pltpu.VMEM((TAPS, 128), F32),
            pltpu.VMEM((8, n_q, 8, 128), F32),
            pltpu.VMEM((8, n_q, 8, 128), F32),
            pltpu.VMEM((n_q, 8, 128), F32),
            pltpu.VMEM((n_q * 4, 8, 128), F32),
        ]
        + [pltpu.VMEM((ROWS, LANES), BF16)] * 4
        + [
            pltpu.SemaphoreType.DMA((4, CHUNKS)),
            pltpu.SemaphoreType.DMA((4, CHUNKS)),
            pltpu.SemaphoreType.DMA((2, CHUNKS)),
            pltpu.SemaphoreType.DMA((2, CHUNKS)),
            pltpu.SemaphoreType.DMA((2, CHUNKS)),
            pltpu.SemaphoreType.DMA((2, CHUNKS)),
            pltpu.SemaphoreType.DMA((8,)),
            pltpu.SemaphoreType.DMA((8,)),
            pltpu.SemaphoreType.DMA((16,)),
            pltpu.SemaphoreType.DMA((16,)),
            pltpu.SemaphoreType.DMA,
        ],
        compiler_params=pltpu.CompilerParams(
            collective_id=0, has_side_effects=True, vmem_limit_bytes=48 * 1024 * 1024
        ),
        cost_estimate=pl.CostEstimate(flops=3 * 10**9, bytes_accessed=4 * 2**20, transcendentals=0),
        name="hyena",
    )(q_proj, k_proj, v_proj, filt, skip.reshape(1, LANES), grad_out)
    return tuple(outs)


def solution(mesh):
    in_specs = (
        P("ctx", "ch"),
        P("ctx", "ch"),
        P("ctx", "ch"),
        P(None, "ch"),
        P("ch"),
        P("ctx", "ch"),
    )
    out_specs = (P("ctx", "ch"), P("ctx", "ch"), P("ctx", "ch"), P("ctx", "ch"), P("ctx", None))
    return jax.shard_map(shards, mesh=mesh, in_specs=in_specs, out_specs=out_specs, check_vma=False)
```

time: 854 us -> 53.8 us (0.06); the launches traced: 843 us -> 53.4 us
  waiting for transfers between devices: 489 us -> 0 us
  local copies, waits for them, and re-layouts: 264 us -> 9.52 us
  Pallas kernels: 0 us -> 43.2 us
  matrix products: 41.5 us -> 0 us
  other arithmetic: 17.8 us -> 0 us
  between operations: 15.1 us -> 0.66 us
  starting transfers between devices: 11 us -> 0 us
    unnamed x2 -> x0, waiting for transfers between devices: 477 us -> none
    reshape x4 -> x0, local copies, waits for them, and re-layouts: 125 us -> none  [the longest x3 89.2 us: shards(): spread[:, :rows * (2 * rows - 1)].reshape(groups, rows, 2 * rows - 1)]
    unnamed x42 -> x17, local copies, waits for them, and re-layouts: 70.5 us -> 9.52 us
    slice x8 -> x0, local copies, waits for them, and re-layouts: 44.4 us -> none  [the longest x1 22.6 us: shards(): widened.reshape(groups, 4 * rows * rows)[:, :rows * (4 * rows - 1)]]
    pallas_call x0 -> x1, Pallas kernels: none -> 43.2 us  [shards(): pl.pallas_call(functools.partial(kernel, n_ctx, scale), out_shape=(big, b...]
    dot_general x7 -> x0, matrix products: 41.5 us -> none  [the longest x3 16.1 us: shards(): jnp.einsum('grs,gks->gkr', tab, dconv_lay, preferred_element_type=jnp.flo...]
    reduce_sum x1 -> x0, other arithmetic: 13 us -> none  [shards(): diagonals = jnp.sum(skewed, axis=1)]
    pad x1 -> x0, local copies, waits for them, and re-layouts: 11.5 us -> none  [shards(): widened = jnp.pad(outer, ((0, 0), (0, 0), (0, rows)))]
  transfers between devices with their start and end apart: 5 -> 0, of which waited for: 2 -> 0; matrix products, arithmetic and copies ran while one was open for 35% -> 0% of each run, Pallas kernels for 0% -> 0%
where the time goes in v1:
time: 53.8 us; the launch traced here: 53.4 us
  Pallas kernels  43.2 us (80%)
  local copies, waits for them, and re-layouts  9.52 us (18%)
  between operations  0.66 us (1%)
    pallas_call x1, Pallas kernels, shards(): pl.pallas_call(functools.partial(kernel, n_ctx, scale), out_shape=(big, b...  43.2 us
    unnamed x17, local copies, waits for them, and re-layouts  9.52 us

profile of v1, /device:TPU:1, one launch (start us, length us, event | category | flops | bytes accessed | tf_op | source)
XLA Modules:
  0.0 53.4 jit_solution(16443038476078811008)
XLA Ops:
  0.6 0.0 copy-start
  0.6 1.0 %copy-done = bf16[128,2048]{1,0:T(8,128)(2,1)S(1)} copy-done((bf16[128,2048]{1,0:T(8,128)(2,1)S(1)}, bf16[128,2048]{1,0:T(8,128)(2,1)}, u32[]{:S(2)}) %copy-start) | copy-done | bytes 524312
  1.7 0.0 copy-start.1
  1.7 1.0 %copy-done.1 = bf16[128,2048]{1,0:T(8,128)(2,1)S(1)} copy-done((bf16[128,2048]{1,0:T(8,128)(2,1)S(1)}, bf16[128,2048]{1,0:T(8,128)(2,1)}, u32[]{:S(2)}) %copy-start.1) | copy-done | bytes 524312
  2.7 0.0 copy-start.2
  2.7 1.0 %copy-done.2 = bf16[128,2048]{1,0:T(8,128)(2,1)S(1)} copy-done((bf16[128,2048]{1,0:T(8,128)(2,1)S(1)}, bf16[128,2048]{1,0:T(8,128)(2,1)}, u32[]{:S(2)}) %copy-start.2) | copy-done | bytes 524312
  3.8 0.0 copy-start.3
  3.8 1.0 %copy-done.3 = bf16[128,2048]{1,0:T(8,128)(2,1)S(1)} copy-done((bf16[128,2048]{1,0:T(8,128)(2,1)S(1)}, bf16[128,2048]{1,0:T(8,128)(2,1)}, u32[]{:S(2)}) %copy-start.3) | copy-done | bytes 524312
  4.8 0.0 copy-start.4
  4.8 0.9 %copy-done.4 = f32[256,128]{1,0:T(8,128)S(1)} copy-done((f32[256,128]{1,0:T(8,128)S(1)}, f32[256,128]{1,0:T(8,128)}, u32[]{:S(2)}) %copy-start.4) | copy-done | bytes 131096
  5.7 0.0 copy-start.5
  5.7 0.7 %copy-done.5 = f32[2048]{0:T(1024)S(1)} copy-done((f32[2048]{0:T(1024)S(1)}, f32[2048]{0:T(1024)}, u32[]{:S(2)}) %copy-start.5) | copy-done | bytes 8216
  6.4 43.2 %hyena.1 = (bf16[128,2048]{1,0:T(8,128)(2,1)S(1)}, bf16[128,2048]{1,0:T(8,128)(2,1)S(1)}, bf16[128,2048]{1,0:T(8,128)(2,1)S(1)}, bf16[128,2048]{1,0:T(8,128)(2,1)S(1)}, f32[4,256]{1,0:T(4,128)S(1)}) custom-call(bf16[128,2048]{1,0:T(8,128)(2,1)S(1)} %copy-done, bf16[128,2048]{1,0:T(8,128)(2,1)S(1)} %copy-done.1, bf16[128,2048]{1,0:T(8,128)(2,1)S(1)} %copy-done.2, ...), custom_call_target="tpu_custom_call" | custom-call | flops 3000000000 | bytes 4194304 | tf_op jit(solution)/shard_map/hyena/pallas_call | solution.py:347
  49.6 0.8 %copy.16 = bf16[128,2048]{1,0:T(8,128)(2,1)} copy(bf16[128,2048]{1,0:T(8,128)(2,1)S(1)} %get-tuple-element.10) | data formatting | bytes 1048576
  50.4 0.8 %copy.17 = bf16[128,2048]{1,0:T(8,128)(2,1)} copy(bf16[128,2048]{1,0:T(8,128)(2,1)S(1)} %get-tuple-element.11) | data formatting | bytes 1048576
  51.2 0.8 %copy.18 = bf16[128,2048]{1,0:T(8,128)(2,1)} copy(bf16[128,2048]{1,0:T(8,128)(2,1)S(1)} %get-tuple-element.12) | data formatting | bytes 1048576
  52.0 0.8 %copy.19 = bf16[128,2048]{1,0:T(8,128)(2,1)} copy(bf16[128,2048]{1,0:T(8,128)(2,1)S(1)} %get-tuple-element.13) | data formatting | bytes 1048576
  52.8 0.6 %copy.20 = f32[4,256]{1,0:T(4,128)} copy(f32[4,256]{1,0:T(4,128)S(1)} %get-tuple-element.14) | data formatting | bytes 8192
Async XLA Ops:
  0.6 1.0 %copy-start = (bf16[128,2048]{1,0:T(8,128)(2,1)S(1)}, bf16[128,2048]{1,0:T(8,128)(2,1)}, u32[]{:S(2)}) copy-start(bf16[128,2048]{1,0:T(8,128)(2,1)} %q_hbm.1) | copy-start | bytes 1572868
  1.7 1.0 %copy-start.1 = (bf16[128,2048]{1,0:T(8,128)(2,1)S(1)}, bf16[128,2048]{1,0:T(8,128)(2,1)}, u32[]{:S(2)}) copy-start(bf16[128,2048]{1,0:T(8,128)(2,1)} %k_hbm.1) | copy-start | bytes 1572868
  2.7 1.0 %copy-start.2 = (bf16[128,2048]{1,0:T(8,128)(2,1)S(1)}, bf16[128,2048]{1,0:T(8,128)(2,1)}, u32[]{:S(2)}) copy-start(bf16[128,2048]{1,0:T(8,128)(2,1)} %v_hbm.1) | copy-start | bytes 1572868
  3.8 1.0 %copy-start.3 = (bf16[128,2048]{1,0:T(8,128)(2,1)S(1)}, bf16[128,2048]{1,0:T(8,128)(2,1)}, u32[]{:S(2)}) copy-start(bf16[128,2048]{1,0:T(8,128)(2,1)} %g_hbm.1) | copy-start | bytes 1572868
  4.8 0.9 %copy-start.4 = (f32[256,128]{1,0:T(8,128)S(1)}, f32[256,128]{1,0:T(8,128)}, u32[]{:S(2)}) copy-start(f32[256,128]{1,0:T(8,128)} %filt_ref.1) | copy-start | bytes 393220
  5.7 0.7 %copy-start.5 = (f32[2048]{0:T(1024)S(1)}, f32[2048]{0:T(1024)}, u32[]{:S(2)}) copy-start(f32[2048]{0:T(1024)} %param.10) | copy-start | bytes 24580

commit v2 on v0

v2 whole, which is shorter than its diff:
```python
import functools

import jax
import jax.numpy as jnp
from jax import lax
from jax.experimental import pallas as pl
from jax.experimental.pallas import tpu as pltpu
from jax.sharding import PartitionSpec as P

MESH = pl.DeviceIdType.MESH
F32 = jnp.float32
BF16 = jnp.bfloat16
ROWS = 128
LANES = 2048
TILES = LANES // 128
CHUNKS = 8
HALF = CHUNKS // 2
PER = TILES // CHUNKS
WIDTH = PER * 128
BLK = 16
NB = ROWS // BLK
TAPS = 256
SPAN = TAPS // BLK + 1
SLOTS = SPAN + 2 * (NB - 1)


def iota(shape, dim):
    return lax.broadcasted_iota(jnp.int32, shape, dim)


def kernel(
    n_ctx, scale,
    q_hbm, k_hbm, v_hbm, filt_hbm, skip_hbm, g_hbm,
    mo_ref, qg_ref, kg_ref, vg_ref, fg_ref,
    q_ref, k_ref, v_ref, g_ref, filt_ref, skip_ref,
    x_ref, dc_ref, s_ref, o_ref, mask_ref, sh_ref,
    d_ref, r1_ref, a1_ref, r2_ref,
    in_sem, small_sem, far_send, far_recv, near_send, near_recv,
    s1_send, s1_recv, s2_send, s2_recv,
):
    d = lax.axis_index("ctx")
    h = lax.axis_index("ch")
    up = lax.rem(d + 2, n_ctx)
    down = lax.rem(d + n_ctx - 2, n_ctx)
    core = lax.rem(d, 2)
    mate = d + 1 - 2 * core
    n_zx = n_ctx // 8
    zx = lax.div(d, 8)
    j = lax.rem(d, 8)
    e = j * 2 + h

    def turn(n, p):
        return (p + HALF) % CHUNKS if n == 0 else p

    def load(n, p):
        src, dst = ((k_hbm, k_ref), (v_hbm, v_ref), (g_hbm, g_ref), (q_hbm, q_ref))[n]
        cols = pl.ds(turn(n // 2, p) * WIDTH, WIDTH)
        return pltpu.make_async_copy(src.at[:, cols], dst.at[:, cols], in_sem.at[n, p])

    for p in range(CHUNKS):
        for n in range(4):
            load(n, p).start()
    load_filt = pltpu.make_async_copy(filt_hbm, filt_ref, small_sem.at[0])
    load_skip = pltpu.make_async_copy(skip_hbm, skip_ref, small_sem.at[1])
    load_filt.start()
    load_skip.start()

    def stage1_peer(step):
        return lax.rem(zx + step, n_zx)

    def stage2_peer(step):
        other = lax.rem(e + step, 16)
        return other, zx * 8 + lax.div(other, 2), lax.rem(other, 2)

    barrier = pltpu.get_barrier_semaphore()
    peers = [(up, h), (down, h)]
    peers += [(stage1_peer(step) * 8 + j, h) for step in range(1, n_zx)]
    peers += [stage2_peer(step)[1:] for step in range(1, 16)]
    for peer in peers:
        pl.semaphore_signal(barrier, inc=1, device_id=peer, device_id_type=MESH)

    flip = (iota((ROWS, ROWS), 0) + iota((ROWS, ROWS), 1) == ROWS - 1).astype(F32).astype(BF16)
    fr, fc = iota((ROWS, 2 * ROWS), 0), iota((ROWS, 2 * ROWS), 1) % ROWS
    flip2 = (jnp.logical_and(fr // BLK == fc // BLK, fr % BLK + fc % BLK == BLK - 1)).astype(F32).astype(BF16)
    for g in range(8):
        mask_ref[g] = (iota((BLK, 128), 1) // BLK == g).astype(F32).astype(BF16)

    def far(n, c):
        ref, target = ((x_ref, up), (dc_ref, down))[n]
        cs = pl.ds(c * PER, PER)
        return pltpu.make_async_remote_copy(
            src_ref=ref.at[0, cs], dst_ref=ref.at[2, cs],
            send_sem=far_send.at[n, c], recv_sem=far_recv.at[n, c],
            device_id=(target, h), device_id_type=MESH,
        )

    def near(n, c, src_slot):
        ref = (x_ref, dc_ref)[n]
        cs = pl.ds(c * PER, PER)
        return pltpu.make_async_remote_copy(
            src_ref=ref.at[src_slot, cs], dst_ref=ref.at[1, cs],
            send_sem=near_send.at[n, c], recv_sem=near_recv.at[n, c],
            device_id=(mate, h), device_id_type=MESH,
        )

    for p in range(CHUNKS):
        c0, c1 = turn(0, p), turn(1, p)
        load(0, p).wait()
        load(1, p).wait()
        cols = pl.ds(c0 * WIDTH, WIDTH)
        st = (k_ref[:, cols].astype(F32) * v_ref[:, cols].astype(F32)).astype(BF16)
        st = jnp.dot(flip, st, preferred_element_type=F32).astype(BF16)
        for t in range(PER):
            x_ref[0, c0 * PER + t] = st[:, t * 128 : (t + 1) * 128]
        load(2, p).wait()
        load(3, p).wait()
        cols = pl.ds(c1 * WIDTH, WIDTH)
        dc = (g_ref[:, cols].astype(F32) * q_ref[:, cols].astype(F32)).astype(BF16)
        for t in range(PER):
            dc_ref[0, c1 * PER + t] = dc[:, t * 128 : (t + 1) * 128]
        if p == 0:
            pl.semaphore_wait(barrier, len(peers))
        far(0, c0).start()
        far(1, c1).start()

        @pl.when(core == 0)
        def _():
            near(0, c0, 0).start()

        @pl.when(core == 1)
        def _():
            near(1, c1, 0).start()

    load_filt.wait()
    load_skip.wait()
    s_ref[:, :, : (NB - 1) * 128] = jnp.zeros((TILES, BLK, (NB - 1) * 128), BF16)
    s_ref[:, :, (NB - 1 + SPAN) * 128 :] = jnp.zeros((TILES, BLK, (NB - 1) * 128), BF16)
    sh_ref[...] = jnp.zeros_like(sh_ref)
    taps = filt_ref[...].astype(BF16)
    amt = 15 - iota((288, 128), 1) % BLK

    def table(c, carry):
        spots = iota((128, 512), 0) == 32 * c + iota((128, 512), 1) // BLK
        f = jnp.dot(taps, spots.astype(F32).astype(BF16), preferred_element_type=F32)
        edge = jnp.zeros((16, 128), F32)
        for t in range(4):
            z = jnp.concatenate([edge, f[:, t * 128 : (t + 1) * 128], edge], axis=0)
            for b in (8, 4, 2, 1):
                sh_ref[t, 8:296] = z
                z = jnp.where((amt & b) != 0, sh_ref[t, 8 - b : 296 - b], z)
            zb = z.astype(BF16)
            for u in range(SPAN):
                s_ref[c * 4 + t, :, (NB - 1 + u) * 128 : (NB + u) * 128] = zb[16 + 16 * u : 32 + 16 * u]
        return carry

    lax.fori_loop(0, TILES // 4, table, 0)

    def spread(block):
        n_u = block.shape[0] // BLK
        wide = block.reshape(n_u, 1, BLK, 128) * mask_ref[...][None]
        return wide.reshape(n_u * 128, 128)

    def operator(n, u0, n_u):
        return jnp.concatenate(
            [s_ref[n, :, (NB - 1 - i + u0) * 128 : (NB - 1 - i + u0 + n_u) * 128] for i in range(NB)], axis=0
        )

    def own(c, carry):
        for t in range(4):
            n = c * 4 + t
            rhs = jnp.concatenate([spread(x_ref[0, n]), spread(dc_ref[0, n])], axis=1)
            o_ref[n] = jnp.dot(operator(n, 0, NB), rhs, preferred_element_type=F32)
        return carry

    amt2 = 15 - iota((264, 128), 1) % BLK

    def filter_terms(p):
        tiles = [(p * PER + t, dc_ref, x_ref) for t in range(PER)]
        tiles += [((p + HALF) * PER + t, x_ref, dc_ref) for t in range(PER)]
        parts, spots = [], []
        for t, (n, long, short) in enumerate(tiles):
            rows = jnp.concatenate([long[0, n], long[1, n], long[2, n]], axis=0)
            lhs = jnp.concatenate([rows[BLK * i : BLK * i + SPAN * BLK] for i in range(NB)], axis=1)
            st = spread(short[0, n])
            rhs = jnp.concatenate([st[(NB - 1 - i) * 128 : (NB - i) * 128] for i in range(NB)], axis=1)
            sh_ref[t, 0:272] = lax.dot_general(lhs, rhs, (((1,), (1,)), ((), ())), preferred_element_type=F32)
        for t, (n, long, short) in enumerate(tiles):
            z = jnp.where((amt2 & 8) != 0, sh_ref[t, 8:272], sh_ref[t, 0:264])
            for b in (4, 2, 1):
                sh_ref[t, 0:264] = z
                z = jnp.where((amt2 & b) != 0, sh_ref[t, b : 264 + b], z)
            z = z[:TAPS]
            hi = z.astype(BF16)
            parts += [hi, (z - hi.astype(F32)).astype(BF16)]
            spot = (iota((256, 128), 1) == 8 * n + iota((256, 128), 0) % 128 // BLK).astype(F32)
            spots.append(spot.astype(BF16))
        terms = jnp.dot(
            jnp.concatenate(parts, axis=1), jnp.concatenate(spots, axis=0), preferred_element_type=F32
        )
        if p == 0:
            d_ref[...] = terms
        else:
            d_ref[...] += terms

    def rest(p):
        tiles = [p * PER + t for t in range(PER)] + [(p + HALF) * PER + t for t in range(PER)]
        his, los = [], []
        for n in tiles:
            rx = jnp.concatenate([spread(x_ref[1, n]), spread(x_ref[2, n])], axis=0)
            rd = jnp.concatenate([spread(dc_ref[1, n]), spread(dc_ref[2, n])], axis=0)
            out = o_ref[n] + jnp.dot(
                operator(n, NB, 2 * NB), jnp.concatenate([rx, rd], axis=1), preferred_element_type=F32
            )
            o_ref[n] = out
            ds = out[:, 128:]
            hi = ds.astype(BF16)
            his.append(hi)
            los.append((ds - hi.astype(F32)).astype(BF16))
        pair = jnp.concatenate([jnp.concatenate(his, axis=1), jnp.concatenate(los, axis=1)], axis=0)
        flipped = jnp.dot(flip2, pair, preferred_element_type=F32)
        for t, n in enumerate(tiles):
            ls = pl.ds(n * 128, 128)
            conv = jnp.concatenate(
                [o_ref[n, BLK * (NB - 1 - i) : BLK * (NB - i), :128] for i in range(NB)], axis=0
            )
            ds = flipped[:, t * 128 : (t + 1) * 128]
            kf, vf = k_ref[:, ls].astype(F32), v_ref[:, ls].astype(F32)
            qf, gf = q_ref[:, ls].astype(F32), g_ref[:, ls].astype(F32)
            skip = skip_ref[:, ls]
            conv = conv + skip * (kf * vf).astype(BF16).astype(F32)
            ds = ds + skip * dc_ref[0, n].astype(F32)
            mo_ref[:, ls] = (qf * conv).astype(BF16)
            qg_ref[:, ls] = (gf * conv).astype(BF16)
            kg_ref[:, ls] = (ds * vf).astype(BF16)
            vg_ref[:, ls] = (ds * kf).astype(BF16)

    def arrive(p):
        c0, c1 = turn(0, p), turn(1, p)
        far(0, c0).wait_recv()

        @pl.when(d < 2)
        def _():
            x_ref[2, pl.ds(c0 * PER, PER)] = jnp.zeros((PER, ROWS, 128), BF16)

        @pl.when(core == 1)
        def _():
            near(0, c0, 2).start()

        far(1, c1).wait_recv()

        @pl.when(d >= n_ctx - 2)
        def _():
            dc_ref[2, pl.ds(c1 * PER, PER)] = jnp.zeros((PER, ROWS, 128), BF16)

        @pl.when(core == 0)
        def _():
            near(1, c1, 2).start()

    def complete(p):
        near(0, turn(0, p), 0).wait_recv()
        near(1, turn(1, p), 0).wait_recv()

    def stage1(step):
        other = stage1_peer(step)
        return pltpu.make_async_remote_copy(
            src_ref=d_ref.at[pl.ds(other * 32, 32)], dst_ref=r1_ref.at[zx],
            send_sem=s1_send.at[step], recv_sem=s1_recv.at[zx],
            device_id=(other * 8 + j, h), device_id_type=MESH,
        )

    def stage1_from(step):
        other = stage1_peer(step)
        return pltpu.make_async_remote_copy(
            src_ref=d_ref.at[pl.ds(other * 32, 32)], dst_ref=r1_ref.at[other],
            send_sem=s1_send.at[step], recv_sem=s1_recv.at[other],
            device_id=(other * 8 + j, h), device_id_type=MESH,
        )

    def stage2(step):
        other, ctx, ch = stage2_peer(step)
        return pltpu.make_async_remote_copy(
            src_ref=a1_ref.at[lax.div(other, 4)], dst_ref=r2_ref.at[e],
            send_sem=s2_send.at[step], recv_sem=s2_recv.at[e],
            device_id=(ctx, ch), device_id_type=MESH,
        )

    def stage2_from(step):
        other, ctx, ch = stage2_peer(step)
        return pltpu.make_async_remote_copy(
            src_ref=a1_ref.at[lax.div(other, 4)], dst_ref=r2_ref.at[other],
            send_sem=s2_send.at[step], recv_sem=s2_recv.at[other],
            device_id=(ctx, ch), device_id_type=MESH,
        )

    lax.fori_loop(0, 2, own, 0)
    arrive(0)
    lax.fori_loop(2, 4, own, 0)
    for p in range(HALF):
        arrive(p + 1)
        complete(p)
        filter_terms(p)
    for step in range(1, n_zx):
        stage1(step).start()
    arrive(HALF + 1)
    complete(HALF)
    rest(0)

    total = d_ref[pl.ds(zx * 32, 32)]
    for step in range(1, n_zx):
        stage1_from(step).wait_recv()
        total = total + r1_ref[stage1_peer(step)]
    total = (total * scale).reshape(4, 8, 128)
    a1_ref[...] = total
    r2_ref[e] = a1_ref[lax.div(j, 2)]
    for step in range(1, 16):
        stage2(step).start()

    for p in range(1, HALF):
        if HALF + p + 1 < CHUNKS:
            arrive(HALF + p + 1)
        complete(HALF + p)
        rest(p)

    for step in range(1, 16):
        stage2_from(step).wait_recv()
    for hh in range(2):
        total = r2_ref[hh]
        for jj in range(1, 8):
            total = total + r2_ref[jj * 2 + hh]
        fg_ref[:, hh * 128 : (hh + 1) * 128] = jnp.where(core == 0, total[:4], total[4:])

    for c in range(CHUNKS):
        for n in range(2):
            far(n, c).wait_send()
            near(n, c, 0).wait_send()
    for step in range(1, n_zx):
        stage1(step).wait_send()
    for step in range(1, 16):
        stage2(step).wait_send()


def hand_over(*refs):
    src, dst, buf = refs[:5], refs[5:10], refs[10:15]
    in_sem, out_sem = refs[15:]
    steps = [(i, pl.ds(c * 512, 512)) for c in range(4) for i in range(4)] + [(4, pl.ds(0, 256))]
    first = [pltpu.make_async_copy(src[i].at[:, c], buf[i].at[:, c], in_sem.at[n]) for n, (i, c) in enumerate(steps)]
    then = [pltpu.make_async_copy(buf[i].at[:, c], dst[i].at[:, c], out_sem.at[n]) for n, (i, c) in enumerate(steps)]
    for copy in first:
        copy.start()
    for copy, onward in zip(first, then):
        copy.wait()
        onward.start()
    for onward in then:
        onward.wait()


def shards(q_proj, k_proj, v_proj, filt, skip, grad_out):
    n_ctx = lax.axis_size("ctx")
    scale = 1.0 / (16.0 * ROWS * n_ctx) ** 0.5
    hbm = pl.BlockSpec(memory_space=pltpu.HBM)
    anywhere = pl.BlockSpec(memory_space=pl.ANY)
    vmem = pl.BlockSpec(memory_space=pltpu.VMEM)
    big = jax.ShapeDtypeStruct((ROWS, LANES), BF16)
    results = (big, big, big, big, jax.ShapeDtypeStruct((4, 256), F32))
    n_zx = n_ctx // 8
    outs = pl.pallas_call(
        functools.partial(kernel, n_ctx, scale),
        out_shape=results,
        in_specs=[hbm] * 6,
        out_specs=(vmem,) * 5,
        scratch_shapes=[pltpu.VMEM((ROWS, LANES), BF16)] * 4
        + [
            pltpu.VMEM((TAPS, 128), F32),
            pltpu.VMEM((1, LANES), F32),
            pltpu.VMEM((3, TILES, ROWS, 128), BF16),
            pltpu.VMEM((3, TILES, ROWS, 128), BF16),
            pltpu.VMEM((TILES, BLK, SLOTS * 128), BF16),
            pltpu.VMEM((TILES, ROWS, 256), F32),
            pltpu.VMEM((8, BLK, 128), BF16),
            pltpu.VMEM((4, 304, 128), F32),
            pltpu.VMEM((TAPS, 128), F32),
            pltpu.VMEM((n_zx, 32, 128), F32),
            pltpu.VMEM((4, 8, 128), F32),
            pltpu.VMEM((16, 8, 128), F32),
            pltpu.SemaphoreType.DMA((4, CHUNKS)),
            pltpu.SemaphoreType.DMA((2,)),
            pltpu.SemaphoreType.DMA((2, CHUNKS)),
            pltpu.SemaphoreType.DMA((2, CHUNKS)),
            pltpu.SemaphoreType.DMA((2, CHUNKS)),
            pltpu.SemaphoreType.DMA((2, CHUNKS)),
            pltpu.SemaphoreType.DMA((n_zx,)),
            pltpu.SemaphoreType.DMA((n_zx,)),
            pltpu.SemaphoreType.DMA((16,)),
            pltpu.SemaphoreType.DMA((16,)),
        ],
        compiler_params=pltpu.CompilerParams(
            collective_id=0, has_side_effects=True, vmem_limit_bytes=60 * 1024 * 1024
        ),
        cost_estimate=pl.CostEstimate(flops=3 * 10**9, bytes_accessed=4 * 2**20, transcendentals=0),
        name="hyena",
    )(q_proj, k_proj, v_proj, filt, skip.reshape(1, LANES), grad_out)
    outs = pl.pallas_call(
        hand_over,
        out_shape=results,
        in_specs=[hbm] * 5,
        out_specs=(hbm,) * 5,
        scratch_shapes=[pltpu.VMEM(r.shape, r.dtype) for r in results] + [pltpu.SemaphoreType.DMA((17,))] * 2,
        compiler_params=pltpu.CompilerParams(vmem_limit_bytes=60 * 1024 * 1024),
        cost_estimate=pl.CostEstimate(flops=0, bytes_accessed=4 * 2**20, transcendentals=0),
        name="hand_over",
    )(*outs)
    return tuple(outs)


def solution(mesh):
    in_specs = (
        P("ctx", "ch"),
        P("ctx", "ch"),
        P("ctx", "ch"),
        P(None, "ch"),
        P("ch"),
        P("ctx", "ch"),
    )
    out_specs = (P("ctx", "ch"), P("ctx", "ch"), P("ctx", "ch"), P("ctx", "ch"), P("ctx", None))
    return jax.shard_map(shards, mesh=mesh, in_specs=in_specs, out_specs=out_specs, check_vma=False)
```

time: 854 us -> 36.8 us (0.04); the launches traced: 843 us -> 36.7 us
  waiting for transfers between devices: 489 us -> 0 us
  local copies, waits for them, and re-layouts: 264 us -> 0 us
  matrix products: 41.5 us -> 0 us
  Pallas kernels: 0 us -> 36 us
  other arithmetic: 17.8 us -> 0 us
  between operations: 15.1 us -> 0.64 us
  starting transfers between devices: 11 us -> 0 us
    unnamed x2 -> x0, waiting for transfers between devices: 477 us -> none
    reshape x4 -> x0, local copies, waits for them, and re-layouts: 125 us -> none  [the longest x3 89.2 us: shards(): spread[:, :rows * (2 * rows - 1)].reshape(groups, rows, 2 * rows - 1)]
    unnamed x42 -> x0, local copies, waits for them, and re-layouts: 70.5 us -> none
    slice x8 -> x0, local copies, waits for them, and re-layouts: 44.4 us -> none  [the longest x1 22.6 us: shards(): widened.reshape(groups, 4 * rows * rows)[:, :rows * (4 * rows - 1)]]
    dot_general x7 -> x0, matrix products: 41.5 us -> none  [the longest x3 16.1 us: shards(): jnp.einsum('grs,gks->gkr', tab, dconv_lay, preferred_element_type=jnp.flo...]
    pallas_call x0 -> x2, Pallas kernels: none -> 36 us  [the longest x1 33.4 us: shards(): pl.pallas_call(functools.partial(kernel, n_ctx, scale), out_shape=results...]
    reduce_sum x1 -> x0, other arithmetic: 13 us -> none  [shards(): diagonals = jnp.sum(skewed, axis=1)]
    pad x1 -> x0, local copies, waits for them, and re-layouts: 11.5 us -> none  [shards(): widened = jnp.pad(outer, ((0, 0), (0, 0), (0, rows)))]
  transfers between devices with their start and end apart: 5 -> 0, of which waited for: 2 -> 0; matrix products, arithmetic and copies ran while one was open for 35% -> 0% of each run, Pallas kernels for 0% -> 0%
where the time goes in v2:
time: 36.8 us; the launch traced here: 36.7 us
  Pallas kernels  36 us (98%)
  between operations  0.64 us (2%)
    pallas_call x1, Pallas kernels, shards(): pl.pallas_call(functools.partial(kernel, n_ctx, scale), out_shape=results...  33.4 us
    pallas_call x1, Pallas kernels, shards(): pl.pallas_call(hand_over, out_shape=results, in_specs=[hbm] * 5, out_spec...  2.6 us

profile of v2, /device:TPU:1, one launch (start us, length us, event | category | flops | bytes accessed | tf_op | source)
XLA Modules:
  0.0 36.7 jit_solution(12018051956650916457)
XLA Ops:
  0.6 33.4 %hyena.1 = (bf16[128,2048]{1,0:T(8,128)(2,1)}, bf16[128,2048]{1,0:T(8,128)(2,1)}, bf16[128,2048]{1,0:T(8,128)(2,1)}, bf16[128,2048]{1,0:T(8,128)(2,1)}, f32[4,256]{1,0:T(4,128)}) custom-call(bf16[128,2048]{1,0:T(8,128)(2,1)} %q_hbm.1, bf16[128,2048]{1,0:T(8,128)(2,1)} %k_hbm.1, bf16[128,2048]{1,0:T(8,128)(2,1)} %v_hbm.1, f32[256,128]{1,0:T(8,128)} %filt_hbm.1, ...), custom_call_target="tpu_custom_call" | custom-call | flops 3000000000 | bytes 4194304 | tf_op jit(solution)/shard_map/hyena/pallas_call | solution.py:366
  34.1 2.6 %hand_over.1 = (bf16[128,2048]{1,0:T(8,128)(2,1)}, bf16[128,2048]{1,0:T(8,128)(2,1)}, bf16[128,2048]{1,0:T(8,128)(2,1)}, bf16[128,2048]{1,0:T(8,128)(2,1)}, f32[4,256]{1,0:T(4,128)}) custom-call(bf16[128,2048]{1,0:T(8,128)(2,1)} %get-tuple-element.10.refs_0_, bf16[128,2048]{1,0:T(8,128)(2,1)} %get-tuple-element.11.refs_1_, ...), custom_call_target="tpu_custom_call" | custom-call | bytes 4194304 | tf_op jit(solution)/shard_map/hand_over/pallas_call | solution.py:402

commit v3 on v2

--- a/solution.py
+++ b/solution.py
@@ -15,6 +15,7 @@
 TILES = LANES // 128
 CHUNKS = 8
 HALF = CHUNKS // 2
+SHEET = 16
 PER = TILES // CHUNKS
 WIDTH = PER * 128
 BLK = 16
@@ -31,11 +32,12 @@
 def kernel(
     n_ctx, scale,
     q_hbm, k_hbm, v_hbm, filt_hbm, skip_hbm, g_hbm,
-    mo_ref, qg_ref, kg_ref, vg_ref, fg_ref,
+    mo_hbm, qg_hbm, kg_hbm, vg_hbm, fg_hbm,
     q_ref, k_ref, v_ref, g_ref, filt_ref, skip_ref,
     x_ref, dc_ref, s_ref, o_ref, mask_ref, sh_ref,
-    d_ref, r1_ref, a1_ref, r2_ref,
-    in_sem, small_sem, far_send, far_recv, near_send, near_recv,
+    d_ref, d1_ref, r1_ref, a1_ref, r2_ref,
+    mo_ref, qg_ref, kg_ref, vg_ref, fg_ref,
+    in_sem, out_sem, small_sem, far_send, far_recv, near_send, near_recv,
     s1_send, s1_recv, s2_send, s2_recv,
 ):
     d = lax.axis_index("ctx")
@@ -44,40 +46,45 @@
     down = lax.rem(d + n_ctx - 2, n_ctx)
     core = lax.rem(d, 2)
     mate = d + 1 - 2 * core
-    n_zx = n_ctx // 8
-    zx = lax.div(d, 8)
-    j = lax.rem(d, 8)
-    e = j * 2 + h
+    layer = lax.div(d, 2 * SHEET)
+    spot = lax.rem(lax.div(d, 2), SHEET)
+    pile = 2 * n_ctx // SHEET
+    e = (layer * 2 + core) * 2 + h
 
     def turn(n, p):
         return (p + HALF) % CHUNKS if n == 0 else p
 
-    def load(n, p):
+    def load(n, part):
         src, dst = ((k_hbm, k_ref), (v_hbm, v_ref), (g_hbm, g_ref), (q_hbm, q_ref))[n]
-        cols = pl.ds(turn(n // 2, p) * WIDTH, WIDTH)
-        return pltpu.make_async_copy(src.at[:, cols], dst.at[:, cols], in_sem.at[n, p])
-
-    for p in range(CHUNKS):
+        first, count = ((0, 1), (1, HALF - 1), (HALF, HALF))[part]
+        cols = pl.ds(turn(n // 2, first) * WIDTH, count * WIDTH)
+        return pltpu.make_async_copy(src.at[:, cols], dst.at[:, cols], in_sem.at[n, part])
+
+    for n in range(4):
+        load(n, 0).start()
+
+    def stage1_peer(step):
+        other = lax.rem(spot + step, SHEET)
+        return other, (layer * SHEET + other) * 2 + core, h
+
+    def stage2_peer(step):
+        other = lax.rem(e + step, pile)
+        ctx = (lax.div(other, 4) * SHEET + spot) * 2 + lax.rem(lax.div(other, 2), 2)
+        return other, ctx, lax.rem(other, 2)
+
+    barrier = pltpu.get_barrier_semaphore()
+    peers = [(up, h), (down, h)]
+    peers += [stage1_peer(step)[1:] for step in range(1, SHEET)]
+    peers += [stage2_peer(step)[1:] for step in range(1, pile)]
+    for peer in peers:
+        pl.semaphore_signal(barrier, inc=1, device_id=peer, device_id_type=MESH)
+    for part in range(1, 3):
         for n in range(4):
-            load(n, p).start()
+            load(n, part).start()
     load_filt = pltpu.make_async_copy(filt_hbm, filt_ref, small_sem.at[0])
     load_skip = pltpu.make_async_copy(skip_hbm, skip_ref, small_sem.at[1])
     load_filt.start()
     load_skip.start()
-
-    def stage1_peer(step):
-        return lax.rem(zx + step, n_zx)
-
-    def stage2_peer(step):
-        other = lax.rem(e + step, 16)
-        return other, zx * 8 + lax.div(other, 2), lax.rem(other, 2)
-
-    barrier = pltpu.get_barrier_semaphore()
-    peers = [(up, h), (down, h)]
-    peers += [(stage1_peer(step) * 8 + j, h) for step in range(1, n_zx)]
-    peers += [stage2_peer(step)[1:] for step in range(1, 16)]
-    for peer in peers:
-        pl.semaphore_signal(barrier, inc=1, device_id=peer, device_id_type=MESH)
 
     flip = (iota((ROWS, ROWS), 0) + iota((ROWS, ROWS), 1) == ROWS - 1).astype(F32).astype(BF16)
     fr, fc = iota((ROWS, 2 * ROWS), 0), iota((ROWS, 2 * ROWS), 1) % ROWS
@@ -90,7 +97,7 @@
         cs = pl.ds(c * PER, PER)
         return pltpu.make_async_remote_copy(
             src_ref=ref.at[0, cs], dst_ref=ref.at[2, cs],
-            send_sem=far_send.at[n, c], recv_sem=far_recv.at[n, c],
+            send_sem=far_send.at[n], recv_sem=far_recv.at[n, c],
             device_id=(target, h), device_id_type=MESH,
         )
 
@@ -99,27 +106,31 @@
         cs = pl.ds(c * PER, PER)
         return pltpu.make_async_remote_copy(
             src_ref=ref.at[src_slot, cs], dst_ref=ref.at[1, cs],
-            send_sem=near_send.at[n, c], recv_sem=near_recv.at[n, c],
+            send_sem=near_send.at[n], recv_sem=near_recv.at[n, c],
             device_id=(mate, h), device_id_type=MESH,
         )
 
-    for p in range(CHUNKS):
+    def gate(p):
         c0, c1 = turn(0, p), turn(1, p)
-        load(0, p).wait()
-        load(1, p).wait()
+        part = {0: 0, 1: 1, HALF: 2}.get(p)
+        if part is not None:
+            load(0, part).wait()
+            load(1, part).wait()
         cols = pl.ds(c0 * WIDTH, WIDTH)
         st = (k_ref[:, cols].astype(F32) * v_ref[:, cols].astype(F32)).astype(BF16)
         st = jnp.dot(flip, st, preferred_element_type=F32).astype(BF16)
         for t in range(PER):
             x_ref[0, c0 * PER + t] = st[:, t * 128 : (t + 1) * 128]
-        load(2, p).wait()
-        load(3, p).wait()
+        if part is not None:
+            load(2, part).wait()
+            load(3, part).wait()
         cols = pl.ds(c1 * WIDTH, WIDTH)
         dc = (g_ref[:, cols].astype(F32) * q_ref[:, cols].astype(F32)).astype(BF16)
         for t in range(PER):
             dc_ref[0, c1 * PER + t] = dc[:, t * 128 : (t + 1) * 128]
-        if p == 0:
-            pl.semaphore_wait(barrier, len(peers))
+
+    def send(p):
+        c0, c1 = turn(0, p), turn(1, p)
         far(0, c0).start()
         far(1, c1).start()
 
@@ -130,6 +141,13 @@
         @pl.when(core == 1)
         def _():
             near(1, c1, 0).start()
+
+    gate(0)
+    pl.semaphore_wait(barrier, len(peers))
+    send(0)
+    for p in range(1, CHUNKS):
+        gate(p)
+        send(p)
 
     load_filt.wait()
     load_skip.wait()
@@ -201,6 +219,11 @@
             d_ref[...] = terms
         else:
             d_ref[...] += terms
+
+    def store(n, c):
+        src, dst = ((mo_ref, mo_hbm), (qg_ref, qg_hbm), (kg_ref, kg_hbm), (vg_ref, vg_hbm))[n]
+        cols = pl.ds(c * WIDTH, WIDTH)
+        return pltpu.make_async_copy(src.at[:, cols], dst.at[:, cols], out_sem.at[n])
 
     def rest(p):
         tiles = [p * PER + t for t in range(PER)] + [(p + HALF) * PER + t for t in range(PER)]
@@ -233,6 +256,9 @@
             qg_ref[:, ls] = (gf * conv).astype(BF16)
             kg_ref[:, ls] = (ds * vf).astype(BF16)
             vg_ref[:, ls] = (ds * kf).astype(BF16)
+        for c in (p, p + HALF):
+            for n in range(4):
+                store(n, c).start()
 
     def arrive(p):
         c0, c1 = turn(0, p), turn(1, p)
@@ -261,113 +287,110 @@
         near(1, turn(1, p), 0).wait_recv()
 
     def stage1(step):
-        other = stage1_peer(step)
+        other, ctx, ch = stage1_peer(step)
         return pltpu.make_async_remote_copy(
-            src_ref=d_ref.at[pl.ds(other * 32, 32)], dst_ref=r1_ref.at[zx],
-            send_sem=s1_send.at[step], recv_sem=s1_recv.at[zx],
-            device_id=(other * 8 + j, h), device_id_type=MESH,
-        )
-
-    def stage1_from(step):
-        other = stage1_peer(step)
-        return pltpu.make_async_remote_copy(
-            src_ref=d_ref.at[pl.ds(other * 32, 32)], dst_ref=r1_ref.at[other],
-            send_sem=s1_send.at[step], recv_sem=s1_recv.at[other],
-            device_id=(other * 8 + j, h), device_id_type=MESH,
+            src_ref=d1_ref.at[other], dst_ref=r1_ref.at[spot],
+            send_sem=s1_send, recv_sem=s1_recv,
+            device_id=(ctx, ch), device_id_type=MESH,
         )
 
     def stage2(step):
         other, ctx, ch = stage2_peer(step)
         return pltpu.make_async_remote_copy(
-            src_ref=a1_ref.at[lax.div(other, 4)], dst_ref=r2_ref.at[e],
-            send_sem=s2_send.at[step], recv_sem=s2_recv.at[e],
+            src_ref=a1_ref.at[lax.div(other, 2)], dst_ref=r2_ref.at[e],
+            send_sem=s2_send, recv_sem=s2_recv,
             device_id=(ctx, ch), device_id_type=MESH,
         )
 
-    def stage2_from(step):
-        other, ctx, ch = stage2_peer(step)
-        return pltpu.make_async_remote_copy(
-            src_ref=a1_ref.at[lax.div(other, 4)], dst_ref=r2_ref.at[other],
-            send_sem=s2_send.at[step], recv_sem=s2_recv.at[other],
-            device_id=(ctx, ch), device_id_type=MESH,
-        )
-
-    lax.fori_loop(0, 2, own, 0)
-    arrive(0)
-    lax.fori_loop(2, 4, own, 0)
+    own(0, 0)
     for p in range(HALF):
-        arrive(p + 1)
-        complete(p)
-        filter_terms(p)
-    for step in range(1, n_zx):
+        arrive(p)
+        if p > 0:
+            complete(p - 1)
+            filter_terms(p - 1)
+    complete(HALF - 1)
+    filter_terms(HALF - 1)
+    for n in range(SHEET):
+        rows = [d_ref[pl.ds(z * 8 * SHEET + 8 * n, 8)] for z in range(pile // 4)]
+        d1_ref[n] = jnp.concatenate(rows, axis=0).astype(BF16)
+    for step in range(1, SHEET):
         stage1(step).start()
-    arrive(HALF + 1)
-    complete(HALF)
+    arrive(4)
+    own(1, 0)
+    own(2, 0)
+    own(3, 0)
+    arrive(5)
+    complete(4)
     rest(0)
-
-    total = d_ref[pl.ds(zx * 32, 32)]
-    for step in range(1, n_zx):
-        stage1_from(step).wait_recv()
-        total = total + r1_ref[stage1_peer(step)]
-    total = (total * scale).reshape(4, 8, 128)
-    a1_ref[...] = total
-    r2_ref[e] = a1_ref[lax.div(j, 2)]
-    for step in range(1, 16):
+    total = jnp.concatenate([d_ref[pl.ds(z * 8 * SHEET + 8 * spot, 8)] for z in range(pile // 4)], axis=0)
+    others = r1_ref.at[pl.ds(0, SHEET - 1)]
+    pltpu.make_async_copy(others, others, s1_recv).wait()
+    for step in range(1, SHEET):
+        total = total + r1_ref[stage1_peer(step)[0]].astype(F32)
+    total = total * scale
+    for n in range(pile // 2):
+        a1_ref[n] = total[4 * n : 4 * n + 4]
+    r2_ref[e] = a1_ref[lax.div(e, 2)]
+    for step in range(1, pile):
         stage2(step).start()
 
-    for p in range(1, HALF):
-        if HALF + p + 1 < CHUNKS:
-            arrive(HALF + p + 1)
-        complete(HALF + p)
-        rest(p)
-
-    for step in range(1, 16):
-        stage2_from(step).wait_recv()
+    arrive(6)
+    complete(5)
+    rest(1)
+    arrive(7)
+    complete(6)
+    rest(2)
+    complete(7)
+    rest(3)
+    rest_of_pile = r2_ref.at[pl.ds(0, pile - 1)]
+    pltpu.make_async_copy(rest_of_pile, rest_of_pile, s2_recv).wait()
     for hh in range(2):
         total = r2_ref[hh]
-        for jj in range(1, 8):
-            total = total + r2_ref[jj * 2 + hh]
-        fg_ref[:, hh * 128 : (hh + 1) * 128] = jnp.where(core == 0, total[:4], total[4:])
-
-    for c in range(CHUNKS):
-        for n in range(2):
-            far(n, c).wait_send()
-            near(n, c, 0).wait_send()
-    for step in range(1, n_zx):
-        stage1(step).wait_send()
-    for step in range(1, 16):
-        stage2(step).wait_send()
+        for n in range(1, pile // 2):
+            total = total + r2_ref[n * 2 + hh]
+        fg_ref[:, hh * 128 : (hh + 1) * 128] = total
+
+    last = pltpu.make_async_copy(fg_ref, fg_hbm, small_sem.at[0])
+    last.start()
+
+    for n, (src, dst) in enumerate(((mo_ref, mo_hbm), (qg_ref, qg_hbm), (kg_ref, kg_hbm), (vg_ref, vg_hbm))):
+        pltpu.make_async_copy(src, dst, out_sem.at[n]).wait()
+    for n in range(2):
+        whole = (x_ref, dc_ref)[n].at[0]
+        pltpu.make_async_copy(whole, whole, far_send.at[n]).wait()
+        pltpu.make_async_copy(whole, whole, near_send.at[n]).wait()
+    pltpu.make_async_copy(others, others, s1_send).wait()
+    pltpu.make_async_copy(rest_of_pile, rest_of_pile, s2_send).wait()
+    last.wait()
 
 
 def hand_over(*refs):
-    src, dst, buf = refs[:5], refs[5:10], refs[10:15]
-    in_sem, out_sem = refs[15:]
-    steps = [(i, pl.ds(c * 512, 512)) for c in range(4) for i in range(4)] + [(4, pl.ds(0, 256))]
-    first = [pltpu.make_async_copy(src[i].at[:, c], buf[i].at[:, c], in_sem.at[n]) for n, (i, c) in enumerate(steps)]
-    then = [pltpu.make_async_copy(buf[i].at[:, c], dst[i].at[:, c], out_sem.at[n]) for n, (i, c) in enumerate(steps)]
+    src, dst, buf, small = refs[:5], refs[5:10], refs[10], refs[11]
+    in_sem, out_sem = refs[12:]
+    place = [buf.at[i] for i in range(4)] + [small]
+    first = [pltpu.make_async_copy(src[i], place[i], in_sem.at[i]) for i in range(5)]
+    then = [pltpu.make_async_copy(place[i], dst[i], out_sem.at[i // 4]) for i in range(5)]
     for copy in first:
         copy.start()
     for copy, onward in zip(first, then):
         copy.wait()
         onward.start()
-    for onward in then:
-        onward.wait()
+    pltpu.make_async_copy(buf, buf, out_sem.at[0]).wait()
+    then[4].wait()
 
 
 def shards(q_proj, k_proj, v_proj, filt, skip, grad_out):
     n_ctx = lax.axis_size("ctx")
     scale = 1.0 / (16.0 * ROWS * n_ctx) ** 0.5
     hbm = pl.BlockSpec(memory_space=pltpu.HBM)
-    anywhere = pl.BlockSpec(memory_space=pl.ANY)
-    vmem = pl.BlockSpec(memory_space=pltpu.VMEM)
     big = jax.ShapeDtypeStruct((ROWS, LANES), BF16)
     results = (big, big, big, big, jax.ShapeDtypeStruct((4, 256), F32))
-    n_zx = n_ctx // 8
+    pile = 2 * n_ctx // SHEET
     outs = pl.pallas_call(
         functools.partial(kernel, n_ctx, scale),
         out_shape=results,
         in_specs=[hbm] * 6,
-        out_specs=(vmem,) * 5,
+        out_specs=(hbm,) * 5,
         scratch_shapes=[pltpu.VMEM((ROWS, LANES), BF16)] * 4
         + [
             pltpu.VMEM((TAPS, 128), F32),
@@ -379,19 +402,25 @@
             pltpu.VMEM((8, BLK, 128), BF16),
             pltpu.VMEM((4, 304, 128), F32),
             pltpu.VMEM((TAPS, 128), F32),
-            pltpu.VMEM((n_zx, 32, 128), F32),
-            pltpu.VMEM((4, 8, 128), F32),
-            pltpu.VMEM((16, 8, 128), F32),
-            pltpu.SemaphoreType.DMA((4, CHUNKS)),
+            pltpu.VMEM((SHEET, 2 * pile, 128), BF16),
+            pltpu.VMEM((SHEET, 2 * pile, 128), BF16),
+            pltpu.VMEM((pile // 2, 4, 128), F32),
+            pltpu.VMEM((pile, 4, 128), F32),
+        ]
+        + [pltpu.VMEM((ROWS, LANES), BF16)] * 4
+        + [
+            pltpu.VMEM((4, 256), F32),
+            pltpu.SemaphoreType.DMA((4, 3)),
+            pltpu.SemaphoreType.DMA((4,)),
+            pltpu.SemaphoreType.DMA((2,)),
             pltpu.SemaphoreType.DMA((2,)),
             pltpu.SemaphoreType.DMA((2, CHUNKS)),
+            pltpu.SemaphoreType.DMA((2,)),
             pltpu.SemaphoreType.DMA((2, CHUNKS)),
-            pltpu.SemaphoreType.DMA((2, CHUNKS)),
-            pltpu.SemaphoreType.DMA((2, CHUNKS)),
-            pltpu.SemaphoreType.DMA((n_zx,)),
-            pltpu.SemaphoreType.DMA((n_zx,)),
-            pltpu.SemaphoreType.DMA((16,)),
-            pltpu.SemaphoreType.DMA((16,)),
+            pltpu.SemaphoreType.DMA,
+            pltpu.SemaphoreType.DMA,
+            pltpu.SemaphoreType.DMA,
+            pltpu.SemaphoreType.DMA,
         ],
         compiler_params=pltpu.CompilerParams(
             collective_id=0, has_side_effects=True, vmem_limit_bytes=60 * 1024 * 1024
@@ -404,7 +433,12 @@
         out_shape=results,
         in_specs=[hbm] * 5,
         out_specs=(hbm,) * 5,
-        scratch_shapes=[pltpu.VMEM(r.shape, r.dtype) for r in results] + [pltpu.SemaphoreType.DMA((17,))] * 2,
+        scratch_shapes=[
+            pltpu.VMEM((4, ROWS, LANES), BF16),
+            pltpu.VMEM((4, 256), F32),
+            pltpu.SemaphoreType.DMA((5,)),
+            pltpu.SemaphoreType.DMA((2,)),
+        ],
         compiler_params=pltpu.CompilerParams(vmem_limit_bytes=60 * 1024 * 1024),
         cost_estimate=pl.CostEstimate(flops=0, bytes_accessed=4 * 2**20, transcendentals=0),
         name="hand_over",

time: 36.8 us -> 33.6 us (0.913)
  Pallas kernels: 36 us -> 32.8 us
    pallas_call x1, Pallas kernels: 33.4 us -> 30.4 us  [shards(): pl.pallas_call(functools.partial(kernel, n_ctx, scale), out_shape=results...]
where the time goes in v3:
time: 33.6 us; the launch traced here: 33.5 us
  Pallas kernels  32.8 us (98%)
  between operations  0.64 us (2%)
    pallas_call x1, Pallas kernels, shards(): pl.pallas_call(functools.partial(kernel, n_ctx, scale), out_shape=results...  30.4 us
    pallas_call x1, Pallas kernels, shards(): pl.pallas_call(hand_over, out_shape=results, in_specs=[hbm] * 5, out_spec...  2.42 us

profile of v3, /device:TPU:1, one launch (start us, length us, event | category | flops | bytes accessed | tf_op | source)
XLA Modules:
  0.0 33.5 jit_solution(17794962467375830788)
XLA Ops:
  0.6 30.4 %hyena.1 = (bf16[128,2048]{1,0:T(8,128)(2,1)}, bf16[128,2048]{1,0:T(8,128)(2,1)}, bf16[128,2048]{1,0:T(8,128)(2,1)}, bf16[128,2048]{1,0:T(8,128)(2,1)}, f32[4,256]{1,0:T(4,128)}) custom-call(bf16[128,2048]{1,0:T(8,128)(2,1)} %q_hbm.1, bf16[128,2048]{1,0:T(8,128)(2,1)} %k_hbm.1, bf16[128,2048]{1,0:T(8,128)(2,1)} %v_hbm.1, f32[256,128]{1,0:T(8,128)} %filt_hbm.1, ...), custom_call_target="tpu_custom_call" | custom-call | flops 3000000000 | bytes 4194304 | tf_op jit(solution)/shard_map/hyena/pallas_call | solution.py:389
  31.1 2.4 %hand_over.1 = (bf16[128,2048]{1,0:T(8,128)(2,1)}, bf16[128,2048]{1,0:T(8,128)(2,1)}, bf16[128,2048]{1,0:T(8,128)(2,1)}, bf16[128,2048]{1,0:T(8,128)(2,1)}, f32[4,256]{1,0:T(4,128)}) custom-call(bf16[128,2048]{1,0:T(8,128)(2,1)} %get-tuple-element.10.refs_0_, bf16[128,2048]{1,0:T(8,128)(2,1)} %get-tuple-element.11.refs_1_, ...), custom_call_target="tpu_custom_call" | custom-call | bytes 4194304 | tf_op jit(solution)/shard_map/hand_over/pallas_call | solution.py:431

commit v4 on v3

--- a/solution.py
+++ b/solution.py
@@ -34,10 +34,10 @@
     q_hbm, k_hbm, v_hbm, filt_hbm, skip_hbm, g_hbm,
     mo_hbm, qg_hbm, kg_hbm, vg_hbm, fg_hbm,
     q_ref, k_ref, v_ref, g_ref, filt_ref, skip_ref,
-    x_ref, dc_ref, s_ref, o_ref, mask_ref, sh_ref,
+    x_ref, dc_ref, m_ref, s_ref, o_ref, mask_ref, sh_ref, z_ref, tsh_ref,
     d_ref, d1_ref, r1_ref, a1_ref, r2_ref,
     mo_ref, qg_ref, kg_ref, vg_ref, fg_ref,
-    in_sem, out_sem, small_sem, far_send, far_recv, near_send, near_recv,
+    in_sem, out_sem, small_sem, far_send, far_recv, near_send, near_recv, mate_send, mate_recv,
     s1_send, s1_recv, s2_send, s2_recv,
 ):
     d = lax.axis_index("ctx")
@@ -129,10 +129,21 @@
         for t in range(PER):
             dc_ref[0, c1 * PER + t] = dc[:, t * 128 : (t + 1) * 128]
 
+    def to_mate(n, p):
+        ref = (x_ref, dc_ref)[n]
+        return pltpu.make_async_remote_copy(
+            src_ref=ref.at[0, pl.ds(turn(n, p) * PER, PER)], dst_ref=m_ref.at[n, pl.ds((p - HALF) * PER, PER)],
+            send_sem=mate_send.at[n], recv_sem=mate_recv.at[n],
+            device_id=(mate, h), device_id_type=MESH,
+        )
+
     def send(p):
         c0, c1 = turn(0, p), turn(1, p)
         far(0, c0).start()
         far(1, c1).start()
+        if p >= HALF:
+            to_mate(0, p).start()
+            to_mate(1, p).start()
 
         @pl.when(core == 0)
         def _():
@@ -149,29 +160,22 @@
         gate(p)
         send(p)
 
-    load_filt.wait()
-    load_skip.wait()
-    s_ref[:, :, : (NB - 1) * 128] = jnp.zeros((TILES, BLK, (NB - 1) * 128), BF16)
-    s_ref[:, :, (NB - 1 + SPAN) * 128 :] = jnp.zeros((TILES, BLK, (NB - 1) * 128), BF16)
-    sh_ref[...] = jnp.zeros_like(sh_ref)
-    taps = filt_ref[...].astype(BF16)
     amt = 15 - iota((288, 128), 1) % BLK
 
     def table(c, carry):
         spots = iota((128, 512), 0) == 32 * c + iota((128, 512), 1) // BLK
-        f = jnp.dot(taps, spots.astype(F32).astype(BF16), preferred_element_type=F32)
+        f = jnp.dot(filt_ref[...].astype(BF16), spots.astype(F32).astype(BF16), preferred_element_type=F32)
         edge = jnp.zeros((16, 128), F32)
         for t in range(4):
             z = jnp.concatenate([edge, f[:, t * 128 : (t + 1) * 128], edge], axis=0)
             for b in (8, 4, 2, 1):
-                sh_ref[t, 8:296] = z
-                z = jnp.where((amt & b) != 0, sh_ref[t, 8 - b : 296 - b], z)
+                tsh_ref[t, 8:296] = z
+                z = jnp.where((amt & b) != 0, tsh_ref[t, 8 - b : 296 - b], z)
             zb = z.astype(BF16)
             for u in range(SPAN):
                 s_ref[c * 4 + t, :, (NB - 1 + u) * 128 : (NB + u) * 128] = zb[16 + 16 * u : 32 + 16 * u]
         return carry
 
-    lax.fori_loop(0, TILES // 4, table, 0)
 
     def spread(block):
         n_u = block.shape[0] // BLK
@@ -191,18 +195,38 @@
         return carry
 
     amt2 = 15 - iota((264, 128), 1) % BLK
+    even, odd = 1.0 - core.astype(F32), core.astype(F32)
+
+    def filter_tiles(p):
+        tiles = [(p * PER + t, dc_ref, x_ref, 0, even) for t in range(PER)]
+        return tiles + [((p + HALF) * PER + t, x_ref, dc_ref, 1, odd) for t in range(PER)]
+
+    def correlate(block, n, short, side):
+        pad = jnp.zeros(((NB - 1) * BLK, 128), BF16)
+        rows = jnp.concatenate([pad, block, pad], axis=0)
+        lhs = jnp.concatenate([rows[BLK * i : BLK * i + (2 * NB - 1) * BLK] for i in range(NB)], axis=1)
+        both = (spread(short[0, n]), spread(m_ref[side, n - side * HALF * PER]))
+        rhs = [jnp.concatenate([b[(NB - 1 - i) * 128 : (NB - i) * 128] for i in range(NB)], axis=1) for b in both]
+        rhs = jnp.concatenate(rhs, axis=0)
+        return lax.dot_general(lhs, rhs, (((1,), (1,)), ((), ())), preferred_element_type=F32)
+
+    def filter_near(p):
+        for n, long, short, side, far_weight in filter_tiles(p):
+            y = correlate(long[0, n], n, short, side)
+            z_ref[n, 0:16] = y[112:128, :128]
+            z_ref[n, 16:128] = y[128:240, :128] + (1.0 - far_weight) * y[0:112, 128:]
+            z_ref[n, 128:256] = (1.0 - far_weight) * y[112:240, 128:]
 
     def filter_terms(p):
-        tiles = [(p * PER + t, dc_ref, x_ref) for t in range(PER)]
-        tiles += [((p + HALF) * PER + t, x_ref, dc_ref) for t in range(PER)]
+        tiles = filter_tiles(p)
         parts, spots = [], []
-        for t, (n, long, short) in enumerate(tiles):
-            rows = jnp.concatenate([long[0, n], long[1, n], long[2, n]], axis=0)
-            lhs = jnp.concatenate([rows[BLK * i : BLK * i + SPAN * BLK] for i in range(NB)], axis=1)
-            st = spread(short[0, n])
-            rhs = jnp.concatenate([st[(NB - 1 - i) * 128 : (NB - i) * 128] for i in range(NB)], axis=1)
-            sh_ref[t, 0:272] = lax.dot_general(lhs, rhs, (((1,), (1,)), ((), ())), preferred_element_type=F32)
-        for t, (n, long, short) in enumerate(tiles):
+        for t, (n, long, short, side, far_weight) in enumerate(tiles):
+            y = correlate(long[2, n], n, short, side)
+            sh_ref[t, 0:16] = z_ref[n, 0:16]
+            sh_ref[t, 16:144] = z_ref[n, 16:144] + far_weight * y[0:128, 128:]
+            sh_ref[t, 144:256] = z_ref[n, 144:256] + far_weight * y[128:240, 128:] + y[0:112, :128]
+            sh_ref[t, 256:272] = y[112:128, :128]
+        for t, (n, long, short, side, far_weight) in enumerate(tiles):
             z = jnp.where((amt2 & 8) != 0, sh_ref[t, 8:272], sh_ref[t, 0:264])
             for b in (4, 2, 1):
                 sh_ref[t, 0:264] = z
@@ -302,23 +326,30 @@
             device_id=(ctx, ch), device_id_type=MESH,
         )
 
-    own(0, 0)
+    for n in range(2):
+        pltpu.make_async_copy(m_ref.at[n], m_ref.at[n], mate_recv.at[n]).wait()
+    filter_near(0)
+    filter_near(1)
     for p in range(HALF):
         arrive(p)
-        if p > 0:
-            complete(p - 1)
-            filter_terms(p - 1)
-    complete(HALF - 1)
-    filter_terms(HALF - 1)
+        filter_terms(p)
+        if p + 2 < HALF:
+            filter_near(p + 2)
     for n in range(SHEET):
         rows = [d_ref[pl.ds(z * 8 * SHEET + 8 * n, 8)] for z in range(pile // 4)]
         d1_ref[n] = jnp.concatenate(rows, axis=0).astype(BF16)
     for step in range(1, SHEET):
         stage1(step).start()
+    for p in range(HALF):
+        complete(p)
+    load_filt.wait()
+    load_skip.wait()
+    s_ref[:, :, : (NB - 1) * 128] = jnp.zeros((TILES, BLK, (NB - 1) * 128), BF16)
+    s_ref[:, :, (NB - 1 + SPAN) * 128 :] = jnp.zeros((TILES, BLK, (NB - 1) * 128), BF16)
+    tsh_ref[...] = jnp.zeros_like(tsh_ref)
+    lax.fori_loop(0, TILES // 4, table, 0)
     arrive(4)
-    own(1, 0)
-    own(2, 0)
-    own(3, 0)
+    lax.fori_loop(0, TILES // 4, own, 0)
     arrive(5)
     complete(4)
     rest(0)
@@ -359,6 +390,7 @@
         whole = (x_ref, dc_ref)[n].at[0]
         pltpu.make_async_copy(whole, whole, far_send.at[n]).wait()
         pltpu.make_async_copy(whole, whole, near_send.at[n]).wait()
+        pltpu.make_async_copy(m_ref.at[n], m_ref.at[n], mate_send.at[n]).wait()
     pltpu.make_async_copy(others, others, s1_send).wait()
     pltpu.make_async_copy(rest_of_pile, rest_of_pile, s2_send).wait()
     last.wait()
@@ -397,9 +429,12 @@
             pltpu.VMEM((1, LANES), F32),
             pltpu.VMEM((3, TILES, ROWS, 128), BF16),
             pltpu.VMEM((3, TILES, ROWS, 128), BF16),
+            pltpu.VMEM((2, TILES // 2, ROWS, 128), BF16),
             pltpu.VMEM((TILES, BLK, SLOTS * 128), BF16),
             pltpu.VMEM((TILES, ROWS, 256), F32),
             pltpu.VMEM((8, BLK, 128), BF16),
+            pltpu.VMEM((4, 272, 128), F32),
+            pltpu.VMEM((TILES, TAPS, 128), F32),
             pltpu.VMEM((4, 304, 128), F32),
             pltpu.VMEM((TAPS, 128), F32),
             pltpu.VMEM((SHEET, 2 * pile, 128), BF16),
@@ -417,6 +452,8 @@
             pltpu.SemaphoreType.DMA((2, CHUNKS)),
             pltpu.SemaphoreType.DMA((2,)),
             pltpu.SemaphoreType.DMA((2, CHUNKS)),
+            pltpu.SemaphoreType.DMA((2,)),
+            pltpu.SemaphoreType.DMA((2,)),
             pltpu.SemaphoreType.DMA,
             pltpu.SemaphoreType.DMA,
             pltpu.SemaphoreType.DMA,

time: 33.6 us -> 33.1 us (0.985)
  Pallas kernels: 32.8 us -> 32.1 us
    pallas_call x1, Pallas kernels: 30.4 us -> 29.7 us  [shards(): pl.pallas_call(functools.partial(kernel, n_ctx, scale), out_shape=results...]
where the time goes in v4:
time: 33.1 us; the launch traced here: 33 us
  Pallas kernels  32.1 us (97%)
  between operations  0.8 us (2%)
    pallas_call x1, Pallas kernels, shards(): pl.pallas_call(functools.partial(kernel, n_ctx, scale), out_shape=results...  29.7 us
    pallas_call x1, Pallas kernels, shards(): pl.pallas_call(hand_over, out_shape=results, in_specs=[hbm] * 5, out_spec...  2.42 us

profile of v4, /device:TPU:1, one launch (start us, length us, event | category | flops | bytes accessed | tf_op | source)
XLA Modules:
  0.0 33.0 jit_solution(9263573455805231148)
XLA Ops:
  0.6 29.7 %hyena.1 = (bf16[128,2048]{1,0:T(8,128)(2,1)}, bf16[128,2048]{1,0:T(8,128)(2,1)}, bf16[128,2048]{1,0:T(8,128)(2,1)}, bf16[128,2048]{1,0:T(8,128)(2,1)}, f32[4,256]{1,0:T(4,128)}) custom-call(bf16[128,2048]{1,0:T(8,128)(2,1)} %q_hbm.1, bf16[128,2048]{1,0:T(8,128)(2,1)} %k_hbm.1, bf16[128,2048]{1,0:T(8,128)(2,1)} %v_hbm.1, f32[256,128]{1,0:T(8,128)} %filt_hbm.1, ...), custom_call_target="tpu_custom_call" | custom-call | flops 3000000000 | bytes 4194304 | tf_op jit(solution)/shard_map/hyena/pallas_call | solution.py:421
  30.4 2.4 %hand_over.1 = (bf16[128,2048]{1,0:T(8,128)(2,1)}, bf16[128,2048]{1,0:T(8,128)(2,1)}, bf16[128,2048]{1,0:T(8,128)(2,1)}, bf16[128,2048]{1,0:T(8,128)(2,1)}, f32[4,256]{1,0:T(4,128)}) custom-call(bf16[128,2048]{1,0:T(8,128)(2,1)} %get-tuple-element.10.refs_0_, bf16[128,2048]{1,0:T(8,128)(2,1)} %get-tuple-element.11.refs_1_, ...), custom_call_target="tpu_custom_call" | custom-call | bytes 4194304 | tf_op jit(solution)/shard_map/hand_over/pallas_call | solution.py:468

commit v5 on v4

--- a/solution.py
+++ b/solution.py
@@ -52,7 +52,7 @@
     e = (layer * 2 + core) * 2 + h
 
     def turn(n, p):
-        return (p + HALF) % CHUNKS if n == 0 else p
+        return (lax.rem(p + HALF, CHUNKS) if not isinstance(p, int) else (p + HALF) % CHUNKS) if n == 0 else p
 
     def load(n, part):
         src, dst = ((k_hbm, k_ref), (v_hbm, v_ref), (g_hbm, g_ref), (q_hbm, q_ref))[n]
@@ -60,8 +60,6 @@
         cols = pl.ds(turn(n // 2, first) * WIDTH, count * WIDTH)
         return pltpu.make_async_copy(src.at[:, cols], dst.at[:, cols], in_sem.at[n, part])
 
-    for n in range(4):
-        load(n, 0).start()
 
     def stage1_peer(step):
         other = lax.rem(spot + step, SHEET)
@@ -78,6 +76,8 @@
     peers += [stage2_peer(step)[1:] for step in range(1, pile)]
     for peer in peers:
         pl.semaphore_signal(barrier, inc=1, device_id=peer, device_id_type=MESH)
+    for n in range(4):
+        load(n, 0).start()
     for part in range(1, 3):
         for n in range(4):
             load(n, part).start()
@@ -112,19 +112,23 @@
 
     def gate(p):
         c0, c1 = turn(0, p), turn(1, p)
-        part = {0: 0, 1: 1, HALF: 2}.get(p)
-        if part is not None:
-            load(0, part).wait()
-            load(1, part).wait()
-        cols = pl.ds(c0 * WIDTH, WIDTH)
+        if isinstance(p, int):
+            for n in range(4):
+                load(n, 0).wait()
+        else:
+            for part, first in ((1, 1), (2, HALF)):
+
+                @pl.when(p == first)
+                def _():
+                    for n in range(4):
+                        load(n, part).wait()
+
+        cols = pl.ds(c0 * WIDTH if isinstance(p, int) else pl.multiple_of(c0 * WIDTH, WIDTH), WIDTH)
         st = (k_ref[:, cols].astype(F32) * v_ref[:, cols].astype(F32)).astype(BF16)
         st = jnp.dot(flip, st, preferred_element_type=F32).astype(BF16)
         for t in range(PER):
             x_ref[0, c0 * PER + t] = st[:, t * 128 : (t + 1) * 128]
-        if part is not None:
-            load(2, part).wait()
-            load(3, part).wait()
-        cols = pl.ds(c1 * WIDTH, WIDTH)
+        cols = pl.ds(c1 * WIDTH if isinstance(p, int) else pl.multiple_of(c1 * WIDTH, WIDTH), WIDTH)
         dc = (g_ref[:, cols].astype(F32) * q_ref[:, cols].astype(F32)).astype(BF16)
         for t in range(PER):
             dc_ref[0, c1 * PER + t] = dc[:, t * 128 : (t + 1) * 128]
@@ -141,9 +145,13 @@
         c0, c1 = turn(0, p), turn(1, p)
         far(0, c0).start()
         far(1, c1).start()
-        if p >= HALF:
-            to_mate(0, p).start()
-            to_mate(1, p).start()
+        if not isinstance(p, int):
+
+            @pl.when(p >= HALF)
+            def _():
+                to_mate(0, p).start()
+                to_mate(1, p).start()
+
 
         @pl.when(core == 0)
         def _():
@@ -156,9 +164,12 @@
     gate(0)
     pl.semaphore_wait(barrier, len(peers))
     send(0)
-    for p in range(1, CHUNKS):
+    def gate_step(p, carry):
         gate(p)
         send(p)
+        return carry
+
+    lax.fori_loop(1, CHUNKS, gate_step, 0)
 
     amt = 15 - iota((288, 128), 1) % BLK
 
@@ -239,14 +250,11 @@
         terms = jnp.dot(
             jnp.concatenate(parts, axis=1), jnp.concatenate(spots, axis=0), preferred_element_type=F32
         )
-        if p == 0:
-            d_ref[...] = terms
-        else:
-            d_ref[...] += terms
+        d_ref[...] += terms
 
     def store(n, c):
         src, dst = ((mo_ref, mo_hbm), (qg_ref, qg_hbm), (kg_ref, kg_hbm), (vg_ref, vg_hbm))[n]
-        cols = pl.ds(c * WIDTH, WIDTH)
+        cols = pl.ds(c * WIDTH if isinstance(c, int) else pl.multiple_of(c * WIDTH, WIDTH), WIDTH)
         return pltpu.make_async_copy(src.at[:, cols], dst.at[:, cols], out_sem.at[n])
 
     def rest(p):
@@ -266,7 +274,7 @@
         pair = jnp.concatenate([jnp.concatenate(his, axis=1), jnp.concatenate(los, axis=1)], axis=0)
         flipped = jnp.dot(flip2, pair, preferred_element_type=F32)
         for t, n in enumerate(tiles):
-            ls = pl.ds(n * 128, 128)
+            ls = pl.ds(n * 128 if isinstance(n, int) else pl.multiple_of(n * 128, 128), 128)
             conv = jnp.concatenate(
                 [o_ref[n, BLK * (NB - 1 - i) : BLK * (NB - i), :128] for i in range(NB)], axis=0
             )
@@ -328,16 +336,21 @@
 
     for n in range(2):
         pltpu.make_async_copy(m_ref.at[n], m_ref.at[n], mate_recv.at[n]).wait()
-    filter_near(0)
-    filter_near(1)
-    for p in range(HALF):
+    def near_step(p, carry):
+        filter_near(p)
+        return carry
+
+    def far_step(p, carry):
         arrive(p)
         filter_terms(p)
-        if p + 2 < HALF:
-            filter_near(p + 2)
+        return carry
+
+    d_ref[...] = jnp.zeros_like(d_ref)
+    lax.fori_loop(0, HALF, near_step, 0)
+    lax.fori_loop(0, HALF, far_step, 0)
     for n in range(SHEET):
         rows = [d_ref[pl.ds(z * 8 * SHEET + 8 * n, 8)] for z in range(pile // 4)]
-        d1_ref[n] = jnp.concatenate(rows, axis=0).astype(BF16)
+        d1_ref[n] = jnp.concatenate(rows, axis=0)
     for step in range(1, SHEET):
         stage1(step).start()
     for p in range(HALF):
@@ -357,7 +370,7 @@
     others = r1_ref.at[pl.ds(0, SHEET - 1)]
     pltpu.make_async_copy(others, others, s1_recv).wait()
     for step in range(1, SHEET):
-        total = total + r1_ref[stage1_peer(step)[0]].astype(F32)
+        total = total + r1_ref[stage1_peer(step)[0]]
     total = total * scale
     for n in range(pile // 2):
         a1_ref[n] = total[4 * n : 4 * n + 4]
@@ -365,14 +378,16 @@
     for step in range(1, pile):
         stage2(step).start()
 
-    arrive(6)
-    complete(5)
-    rest(1)
-    arrive(7)
-    complete(6)
-    rest(2)
-    complete(7)
-    rest(3)
+    def rest_step(p, carry):
+        @pl.when(p + 1 < HALF)
+        def _():
+            arrive(p + HALF + 1)
+
+        complete(p + HALF)
+        rest(p)
+        return carry
+
+    lax.fori_loop(1, HALF, rest_step, 0)
     rest_of_pile = r2_ref.at[pl.ds(0, pile - 1)]
     pltpu.make_async_copy(rest_of_pile, rest_of_pile, s2_recv).wait()
     for hh in range(2):
@@ -437,8 +452,8 @@
             pltpu.VMEM((TILES, TAPS, 128), F32),
             pltpu.VMEM((4, 304, 128), F32),
             pltpu.VMEM((TAPS, 128), F32),
-            pltpu.VMEM((SHEET, 2 * pile, 128), BF16),
-            pltpu.VMEM((SHEET, 2 * pile, 128), BF16),
+            pltpu.VMEM((SHEET, 2 * pile, 128), F32),
+            pltpu.VMEM((SHEET, 2 * pile, 128), F32),
             pltpu.VMEM((pile // 2, 4, 128), F32),
             pltpu.VMEM((pile, 4, 128), F32),
         ]

time: 33.1 us -> 32.8 us (level)
  no operation moved by 1% of the time
where the time goes in v5:
time: 32.8 us; the launch traced here: 32.7 us
  Pallas kernels  32 us (98%)
  between operations  0.64 us (2%)
    pallas_call x1, Pallas kernels, shards(): pl.pallas_call(functools.partial(kernel, n_ctx, scale), out_shape=results...  29.6 us
    pallas_call x1, Pallas kernels, shards(): pl.pallas_call(hand_over, out_shape=results, in_specs=[hbm] * 5, out_spec...  2.42 us

profile of v5, /device:TPU:1, one launch (start us, length us, event | category | flops | bytes accessed | tf_op | source)
XLA Modules:
  0.0 32.7 jit_solution(10575681544126042106)
XLA Ops:
  0.6 29.6 %hyena.1 = (bf16[128,2048]{1,0:T(8,128)(2,1)}, bf16[128,2048]{1,0:T(8,128)(2,1)}, bf16[128,2048]{1,0:T(8,128)(2,1)}, bf16[128,2048]{1,0:T(8,128)(2,1)}, f32[4,256]{1,0:T(4,128)}) custom-call(bf16[128,2048]{1,0:T(8,128)(2,1)} %q_hbm.1, bf16[128,2048]{1,0:T(8,128)(2,1)} %k_hbm.1, bf16[128,2048]{1,0:T(8,128)(2,1)} %v_hbm.1, f32[256,128]{1,0:T(8,128)} %filt_hbm.1, ...), custom_call_target="tpu_custom_call" | custom-call | flops 3000000000 | bytes 4194304 | tf_op jit(solution)/shard_map/hyena/pallas_call | solution.py:436
  30.3 2.4 %hand_over.1 = (bf16[128,2048]{1,0:T(8,128)(2,1)}, bf16[128,2048]{1,0:T(8,128)(2,1)}, bf16[128,2048]{1,0:T(8,128)(2,1)}, bf16[128,2048]{1,0:T(8,128)(2,1)}, f32[4,256]{1,0:T(4,128)}) custom-call(bf16[128,2048]{1,0:T(8,128)(2,1)} %get-tuple-element.10.refs_0_, bf16[128,2048]{1,0:T(8,128)(2,1)} %get-tuple-element.11.refs_1_, ...), custom_call_target="tpu_custom_call" | custom-call | bytes 4194304 | tf_op jit(solution)/shard_map/hand_over/pallas_call | solution.py:483

commit v6 on v5

--- a/solution.py
+++ b/solution.py
@@ -106,7 +106,7 @@
         cs = pl.ds(c * PER, PER)
         return pltpu.make_async_remote_copy(
             src_ref=ref.at[src_slot, cs], dst_ref=ref.at[1, cs],
-            send_sem=near_send.at[n], recv_sem=near_recv.at[n, c],
+            send_sem=near_send.at[n], recv_sem=near_recv.at[n, lax.rem(c, HALF)],
             device_id=(mate, h), device_id_type=MESH,
         )
 
@@ -315,8 +315,9 @@
             near(1, c1, 2).start()
 
     def complete(p):
-        near(0, turn(0, p), 0).wait_recv()
-        near(1, turn(1, p), 0).wait_recv()
+        for n in range(2):
+            two = (x_ref, dc_ref)[n].at[1, pl.ds(0, 2 * PER)]
+            pltpu.make_async_copy(two, two, near_recv.at[n, p]).wait()
 
     def stage1(step):
         other, ctx, ch = stage1_peer(step)
@@ -353,8 +354,6 @@
         d1_ref[n] = jnp.concatenate(rows, axis=0)
     for step in range(1, SHEET):
         stage1(step).start()
-    for p in range(HALF):
-        complete(p)
     load_filt.wait()
     load_skip.wait()
     s_ref[:, :, : (NB - 1) * 128] = jnp.zeros((TILES, BLK, (NB - 1) * 128), BF16)
@@ -364,7 +363,7 @@
     arrive(4)
     lax.fori_loop(0, TILES // 4, own, 0)
     arrive(5)
-    complete(4)
+    complete(0)
     rest(0)
     total = jnp.concatenate([d_ref[pl.ds(z * 8 * SHEET + 8 * spot, 8)] for z in range(pile // 4)], axis=0)
     others = r1_ref.at[pl.ds(0, SHEET - 1)]
@@ -383,7 +382,7 @@
         def _():
             arrive(p + HALF + 1)
 
-        complete(p + HALF)
+        complete(p)
         rest(p)
         return carry
 
@@ -466,7 +465,7 @@
             pltpu.SemaphoreType.DMA((2,)),
             pltpu.SemaphoreType.DMA((2, CHUNKS)),
             pltpu.SemaphoreType.DMA((2,)),
-            pltpu.SemaphoreType.DMA((2, CHUNKS)),
+            pltpu.SemaphoreType.DMA((2, HALF)),
             pltpu.SemaphoreType.DMA((2,)),
             pltpu.SemaphoreType.DMA((2,)),
             pltpu.SemaphoreType.DMA,

time: 32.8 us -> 32.8 us (level)
  no operation moved by 1% of the time
where the time goes in v6:
time: 32.8 us; the launch traced here: 32.6 us
  Pallas kernels  32 us (98%)
  between operations  0.64 us (2%)
    pallas_call x1, Pallas kernels, shards(): pl.pallas_call(functools.partial(kernel, n_ctx, scale), out_shape=results...  29.5 us
    pallas_call x1, Pallas kernels, shards(): pl.pallas_call(hand_over, out_shape=results, in_specs=[hbm] * 5, out_spec...  2.42 us

profile of v6, /device:TPU:1, one launch (start us, length us, event | category | flops | bytes accessed | tf_op | source)
XLA Modules:
  0.0 32.6 jit_solution(9945589672229846254)
XLA Ops:
  0.6 29.5 %hyena.1 = (bf16[128,2048]{1,0:T(8,128)(2,1)}, bf16[128,2048]{1,0:T(8,128)(2,1)}, bf16[128,2048]{1,0:T(8,128)(2,1)}, bf16[128,2048]{1,0:T(8,128)(2,1)}, f32[4,256]{1,0:T(4,128)}) custom-call(bf16[128,2048]{1,0:T(8,128)(2,1)} %q_hbm.1, bf16[128,2048]{1,0:T(8,128)(2,1)} %k_hbm.1, bf16[128,2048]{1,0:T(8,128)(2,1)} %v_hbm.1, f32[256,128]{1,0:T(8,128)} %filt_hbm.1, ...), custom_call_target="tpu_custom_call" | custom-call | flops 3000000000 | bytes 4194304 | tf_op jit(solution)/shard_map/hyena/pallas_call | solution.py:435
  30.2 2.4 %hand_over.1 = (bf16[128,2048]{1,0:T(8,128)(2,1)}, bf16[128,2048]{1,0:T(8,128)(2,1)}, bf16[128,2048]{1,0:T(8,128)(2,1)}, bf16[128,2048]{1,0:T(8,128)(2,1)}, f32[4,256]{1,0:T(4,128)}) custom-call(bf16[128,2048]{1,0:T(8,128)(2,1)} %get-tuple-element.10.refs_0_, bf16[128,2048]{1,0:T(8,128)(2,1)} %get-tuple-element.11.refs_1_, ...), custom_call_target="tpu_custom_call" | custom-call | bytes 4194304 | tf_op jit(solution)/shard_map/hand_over/pallas_call | solution.py:482

commit v7 on v6

--- a/solution.py
+++ b/solution.py
@@ -33,13 +33,14 @@
     n_ctx, scale,
     q_hbm, k_hbm, v_hbm, filt_hbm, skip_hbm, g_hbm,
     mo_hbm, qg_hbm, kg_hbm, vg_hbm, fg_hbm,
-    q_ref, k_ref, v_ref, g_ref, filt_ref, skip_ref,
+    in_ref, filt_ref, skip_ref,
     x_ref, dc_ref, m_ref, s_ref, o_ref, mask_ref, sh_ref, z_ref, tsh_ref,
     d_ref, d1_ref, r1_ref, a1_ref, r2_ref,
     mo_ref, qg_ref, kg_ref, vg_ref, fg_ref,
     in_sem, out_sem, small_sem, far_send, far_recv, near_send, near_recv, mate_send, mate_recv,
     s1_send, s1_recv, s2_send, s2_recv,
 ):
+    q_ref, k_ref, v_ref, g_ref = (in_ref.at[n] for n in range(4))
     d = lax.axis_index("ctx")
     h = lax.axis_index("ch")
     up = lax.rem(d + 2, n_ctx)
@@ -58,8 +59,12 @@
         src, dst = ((k_hbm, k_ref), (v_hbm, v_ref), (g_hbm, g_ref), (q_hbm, q_ref))[n]
         first, count = ((0, 1), (1, HALF - 1), (HALF, HALF))[part]
         cols = pl.ds(turn(n // 2, first) * WIDTH, count * WIDTH)
-        return pltpu.make_async_copy(src.at[:, cols], dst.at[:, cols], in_sem.at[n, part])
-
+        return pltpu.make_async_copy(src.at[:, cols], dst.at[:, cols], in_sem.at[part])
+
+
+    def loaded(part):
+        four = in_ref.at[:, :, pl.ds(0, (1, HALF - 1, HALF)[part] * WIDTH)]
+        pltpu.make_async_copy(four, four, in_sem.at[part]).wait()
 
     def stage1_peer(step):
         other = lax.rem(spot + step, SHEET)
@@ -113,15 +118,13 @@
     def gate(p):
         c0, c1 = turn(0, p), turn(1, p)
         if isinstance(p, int):
-            for n in range(4):
-                load(n, 0).wait()
+            loaded(0)
         else:
             for part, first in ((1, 1), (2, HALF)):
 
                 @pl.when(p == first)
                 def _():
-                    for n in range(4):
-                        load(n, part).wait()
+                    loaded(part)
 
         cols = pl.ds(c0 * WIDTH if isinstance(p, int) else pl.multiple_of(c0 * WIDTH, WIDTH), WIDTH)
         st = (k_ref[:, cols].astype(F32) * v_ref[:, cols].astype(F32)).astype(BF16)
@@ -437,8 +440,8 @@
         out_shape=results,
         in_specs=[hbm] * 6,
         out_specs=(hbm,) * 5,
-        scratch_shapes=[pltpu.VMEM((ROWS, LANES), BF16)] * 4
-        + [
+        scratch_shapes=[
+            pltpu.VMEM((4, ROWS, LANES), BF16),
             pltpu.VMEM((TAPS, 128), F32),
             pltpu.VMEM((1, LANES), F32),
             pltpu.VMEM((3, TILES, ROWS, 128), BF16),
@@ -459,7 +462,7 @@
         + [pltpu.VMEM((ROWS, LANES), BF16)] * 4
         + [
             pltpu.VMEM((4, 256), F32),
-            pltpu.SemaphoreType.DMA((4, 3)),
+            pltpu.SemaphoreType.DMA((3,)),
             pltpu.SemaphoreType.DMA((4,)),
             pltpu.SemaphoreType.DMA((2,)),
             pltpu.SemaphoreType.DMA((2,)),

time: 32.8 us -> 32.7 us (level)
  no operation moved by 1% of the time
where the time goes in v7:
time: 32.7 us; the launch traced here: 32.5 us
  Pallas kernels  31.9 us (98%)
  between operations  0.64 us (2%)
    pallas_call x1, Pallas kernels, shards(): pl.pallas_call(functools.partial(kernel, n_ctx, scale), out_shape=results...  29.5 us
    pallas_call x1, Pallas kernels, shards(): pl.pallas_call(hand_over, out_shape=results, in_specs=[hbm] * 5, out_spec...  2.42 us

profile of v7, /device:TPU:1, one launch (start us, length us, event | category | flops | bytes accessed | tf_op | source)
XLA Modules:
  0.0 32.5 jit_solution(3817798514461089380)
XLA Ops:
  0.6 29.5 %hyena.1 = (bf16[128,2048]{1,0:T(8,128)(2,1)}, bf16[128,2048]{1,0:T(8,128)(2,1)}, bf16[128,2048]{1,0:T(8,128)(2,1)}, bf16[128,2048]{1,0:T(8,128)(2,1)}, f32[4,256]{1,0:T(4,128)}) custom-call(bf16[128,2048]{1,0:T(8,128)(2,1)} %q_hbm.1, bf16[128,2048]{1,0:T(8,128)(2,1)} %k_hbm.1, bf16[128,2048]{1,0:T(8,128)(2,1)} %v_hbm.1, f32[256,128]{1,0:T(8,128)} %filt_hbm.1, ...), custom_call_target="tpu_custom_call" | custom-call | flops 3000000000 | bytes 4194304 | tf_op jit(solution)/shard_map/hyena/pallas_call | solution.py:438
  30.1 2.4 %hand_over.1 = (bf16[128,2048]{1,0:T(8,128)(2,1)}, bf16[128,2048]{1,0:T(8,128)(2,1)}, bf16[128,2048]{1,0:T(8,128)(2,1)}, bf16[128,2048]{1,0:T(8,128)(2,1)}, f32[4,256]{1,0:T(4,128)}) custom-call(bf16[128,2048]{1,0:T(8,128)(2,1)} %get-tuple-element.10.refs_0_, bf16[128,2048]{1,0:T(8,128)(2,1)} %get-tuple-element.11.refs_1_, ...), custom_call_target="tpu_custom_call" | custom-call | bytes 4194304 | tf_op jit(solution)/shard_map/hand_over/pallas_call | solution.py:485
